TPU v7x, 512 devices: a whole 4x8x8 slice. The times are simulated.
512 devices in a mesh: gx: 16 (over z_hi, x, core), gy: 32 (over y, z_lo).
Axes of the slice: x: 4, y: 8, z: 8 (z_hi: 2, z_lo: 4; z = z_hi * 4 + z_lo), core: 2. Of those that a mesh axis runs over, the one named last changes fastest.
Arguments:
- grid_field: bfloat16 [1, 4, 16, 128, 128, 128], P(None, None, None, 'gx', 'gy'), may hold values from -6 to 6
- spectral_weight: bfloat16 [16, 16, 64, 32, 512], P(None, None, 'gx', 'gy'), may hold values from -3 to 3
- point_weight: bfloat16 [16, 16], replicated, may hold values from -1.5 to 1.5
- cotangent: bfloat16 [1, 4, 16, 128, 128, 128], P(None, None, None, 'gx', 'gy'), may hold values from -6 to 6
Outputs:
- layer_out: bfloat16 [1, 4, 16, 128, 128, 128], P(None, None, None, 'gx', 'gy')
- grad_field: bfloat16 [1, 4, 16, 128, 128, 128], P(None, None, None, 'gx', 'gy')
- grad_spectral: bfloat16 [16, 16, 64, 32, 512], P(None, None, 'gx', 'gy')
All inputs are finite; a program needn't handle non-finite values.
Results may differ from a plain program's by a relative error of at most 0.022.
Values may be sent and summed in bfloat16 or wider, within the bound.
No kernel may reach another device: no remote copies, remote signals or barrier semaphores. Data moves between devices by JAX's collectives and lax.ppermute only.
A program may use at most 128 MiB of HBM per device.

v0:
```python
import math

import jax
import jax.numpy as jnp
import numpy as np
from jax import lax
from jax.experimental import pallas as pl
from jax.experimental.pallas import tpu as pltpu
from jax.sharding import PartitionSpec as P

T = 4
C = 16
X = 128
Y = 128
Z = 128
MX = 64
MY = 64
MZ = 32
GX = 16
GY = 32
XL = X // GX
YL = Y // GY
JL = MY // GX
LANES = 128

F32 = jnp.float32
BF16 = jnp.bfloat16

root_two_over_pi = math.sqrt(2.0 / math.pi)
gelu_cubic = 0.044715


def signed(kept):
    j = np.arange(kept)
    return np.where(j < kept // 2, j, j - kept)


def cos_sin(freq, length):
    q = np.mod(freq[:, None] * np.arange(length)[None, :], length)
    angle = q * (2.0 * np.pi / length)
    return np.cos(angle).astype(BF16), np.sin(angle).astype(BF16)


def tables():
    cz, sz = (a.astype(np.float64) for a in cos_sin(np.arange(MZ), Z))
    quarter = np.mod(np.arange(T)[:, None] * np.arange(T)[None, :], T)
    ct = np.array([1.0, 0.0, -1.0, 0.0])[quarter]
    st = np.array([0.0, 1.0, 0.0, -1.0])[quarter]
    both_cos = (
        cz[None, :, None, :] * ct[:, None, :, None] - sz[None, :, None, :] * st[:, None, :, None]
    )
    both_sin = (
        sz[None, :, None, :] * ct[:, None, :, None] + cz[None, :, None, :] * st[:, None, :, None]
    )
    zt_fwd = np.stack([both_cos, -both_sin], 1).reshape(T * 2 * MZ, T * Z)
    zt_bwd = zt_fwd

    cy, sy = (a.astype(np.float64) for a in cos_sin(signed(MY), Y))
    fwd = np.empty((MY, 2, Y, 2))
    fwd[:, 0, :, 0] = cy
    fwd[:, 0, :, 1] = sy
    fwd[:, 1, :, 0] = -sy
    fwd[:, 1, :, 1] = cy
    y_fwd = fwd.reshape(GX, JL, 2, Y * 2).transpose(1, 2, 0, 3).reshape(MY * 2, Y * 2)
    bwd = np.empty((Y, 2, MY, 2))
    bwd[:, 0, :, 0] = cy.T
    bwd[:, 0, :, 1] = -sy.T
    bwd[:, 1, :, 0] = sy.T
    bwd[:, 1, :, 1] = cy.T
    y_bwd = bwd.reshape(Y * 2, MY * 2)

    cx, sx = (a.astype(np.float64) for a in cos_sin(signed(MX), X))
    fwd = np.empty((X, 2, 2, MX))
    fwd[:, 0, 0, :] = cx.T
    fwd[:, 1, 0, :] = sx.T
    fwd[:, 0, 1, :] = -sx.T
    fwd[:, 1, 1, :] = cx.T
    x_fwd = fwd.reshape(X * 2, 2 * MX)
    bwd = np.empty((X, 2, 2, MX))
    bwd[:, 0, 0, :] = cx.T
    bwd[:, 0, 1, :] = -sx.T
    bwd[:, 1, 0, :] = sx.T
    bwd[:, 1, 1, :] = cx.T
    x_bwd = bwd.reshape(GX, XL, 2, 2 * MX).transpose(1, 2, 0, 3).reshape(X * 2, 2 * MX)
    return tuple(a.astype(BF16) for a in (zt_fwd, zt_bwd, y_fwd, y_bwd, x_fwd, x_bwd))


def dot(left, right, left_dim=1, right_dim=0):
    return lax.dot_general(
        left, right, (((left_dim,), (right_dim,)), ((), ())), preferred_element_type=F32
    )


def swap_bit(low, high, step):
    lane = lax.broadcasted_iota(jnp.int32, low.shape, 1)
    upper = (lane & step) != 0
    first = jnp.where(upper, pltpu.roll(high, step, 1), low)
    second = jnp.where(upper, high, pltpu.roll(low, LANES - step, 1))
    return first, second


def swap_eight(parts):
    parts = list(parts)
    for step in (1, 2, 4):
        for i in range(8):
            if not i & step:
                parts[i], parts[i | step] = swap_bit(parts[i], parts[i | step], step)
    return parts


def gelu_parts(pre):
    inner = root_two_over_pi * (pre + gelu_cubic * pre * pre * pre)
    hyper = jnp.tanh(inner)
    value = 0.5 * pre * (1.0 + hyper)
    slope = 0.5 * (1.0 + hyper) + 0.5 * pre * (1.0 - hyper * hyper) * root_two_over_pi * (
        1.0 + 3.0 * gelu_cubic * pre * pre
    )
    return value, slope


def cells_of(wide_ref, y):
    return jnp.concatenate(
        [wide_ref[pl.ds(t * C * XL * YL + y, C * XL, stride=YL), :] for t in range(T)], 1
    )


def put_cells(wide_ref, y, value):
    for t in range(T):
        wide_ref[pl.ds(t * C * XL * YL + y, C * XL, stride=YL), :] = value[:, t * Z : (t + 1) * Z]


def pack(spread_ref, out_ref):
    for k in range(spread_ref.shape[0]):
        out_ref[:, k * LANES : (k + 1) * LANES] = spread_ref[k].astype(BF16)


def unpack(in_ref, spread_ref):
    for k in range(spread_ref.shape[0]):
        spread_ref[k] = in_ref[:, k * LANES : (k + 1) * LANES].astype(F32)


def put_modes(spread_ref, y, cells, zt_fwd):
    turned = dot(zt_fwd, cells, 1, 1)
    for kt in range(T):
        for p in range(2):
            row = (kt * 2 + p) * MZ
            spread_ref[kt, pl.ds(y * 2 + p, MZ, stride=2 * YL), :] = turned[row : row + MZ]


def modes_of(spread_ref, y):
    return jnp.concatenate(
        [
            spread_ref[kt, pl.ds(y * 2 + p, MZ, stride=2 * YL), :]
            for kt in range(T)
            for p in range(2)
        ],
        0,
    )


def open_kernel(field_ref, zt_ref, out_ref, wide, spread):
    wide[...] = field_ref[...].astype(F32)
    for y in range(YL):
        put_modes(spread, y, cells_of(wide, y).astype(BF16), zt_ref[...])
    pack(spread, out_ref)


def y_forward_kernel(in_ref, table_ref, out_ref, spread):
    along_y = dot(table_ref[...], in_ref[...])
    for low in range(2):
        parts = [
            along_y[
                j * 2 * GX : (j + 1) * 2 * GX,
                (kth * 2 + low) * LANES : (kth * 2 + low + 1) * LANES,
            ]
            for kth in range(2)
            for j in range(JL)
        ]
        for x, part in enumerate(swap_eight(parts)):
            for s in range(2):
                spread[low, pl.ds(x * 2 + s, GX, stride=2 * XL), :] = part[s * GX : (s + 1) * GX]
    pack(spread, out_ref)


def to_spectrum(in_ref, x_fwd_ref):
    low, high = (
        dot(in_ref[:, k * LANES : (k + 1) * LANES], x_fwd_ref[...], 0, 0)
        .astype(BF16)
        .astype(F32)
        for k in range(2)
    )
    return swap_bit(low, high, MX)


def from_spectrum(real, imag, x_bwd_ref, out_ref, spread):
    for low, modes in enumerate(swap_bit(real, imag, MX)):
        along_x = dot(x_bwd_ref[...], modes.astype(BF16), 1, 1)
        parts = [along_x[x * 2 * GX : (x + 1) * 2 * GX] for x in range(XL)]
        for i, part in enumerate(swap_eight(parts)):
            kth, j = divmod(i, JL)
            for s in range(2):
                spread[kth * 2 + low, pl.ds(j * 2 + s, GX, stride=2 * JL), :] = part[
                    s * GX : (s + 1) * GX
                ]
    pack(spread, out_ref)


def weight_parts(w_ref, c):
    w = w_ref[c].astype(F32).reshape(C, 2, 8, LANES)
    return w[:, 0], w[:, 1]


def at_channel(ref, c):
    return ref[pl.ds(pl.multiple_of(c * 8, 8), 8), :]


def mix_kernel(
    in_ref, w_ref, scale_ref, x_fwd_ref, x_bwd_ref, out_ref, real_ref, imag_ref, spread
):
    real, imag = to_spectrum(in_ref, x_fwd_ref)
    real_ref[...] = real
    imag_ref[...] = imag

    def add(c, total):
        s_real = at_channel(real_ref, c)[None]
        s_imag = at_channel(imag_ref, c)[None]
        w_real, w_imag = weight_parts(w_ref, c)
        return (
            total[0] + (s_real * w_real - s_imag * w_imag),
            total[1] + (s_real * w_imag + s_imag * w_real),
        )

    zero = jnp.zeros((C, 8, LANES), F32)
    mix_real, mix_imag = lax.fori_loop(0, C, add, (zero, zero))
    scale = scale_ref[0]
    from_spectrum(
        (mix_real * scale).reshape(C * 8, LANES),
        (mix_imag * scale).reshape(C * 8, LANES),
        x_bwd_ref,
        out_ref,
        spread,
    )


def back_kernel(
    in_ref,
    w_ref,
    scale_ref,
    x_fwd_ref,
    x_bwd_ref,
    out_ref,
    real_ref,
    imag_ref,
    back_real,
    back_imag,
    spread,
):
    real, imag = to_spectrum(in_ref, x_fwd_ref)
    real_ref[...] = real
    imag_ref[...] = imag

    def one(c, carry):
        a_real = real_ref[...].reshape(C, 8, LANES)
        a_imag = imag_ref[...].reshape(C, 8, LANES)
        w_real, w_imag = weight_parts(w_ref, c)
        row = pl.ds(pl.multiple_of(c * 8, 8), 8)
        back_real[row, :] = jnp.sum(a_real * w_real + a_imag * w_imag, 0)
        back_imag[row, :] = jnp.sum(a_imag * w_real - a_real * w_imag, 0)
        return carry

    lax.fori_loop(0, C, one, 0)
    scale = scale_ref[0]
    from_spectrum(back_real[...] * scale, back_imag[...] * scale, x_bwd_ref, out_ref, spread)


def grad_kernel(s_real_ref, s_imag_ref, a_real_ref, a_imag_ref, scale_ref, out_ref):
    def one(c, carry):
        s_real = (at_channel(s_real_ref, c) * scale_ref[0])[None]
        s_imag = (at_channel(s_imag_ref, c) * scale_ref[0])[None]
        a_real = a_real_ref[...].reshape(C, 1, 8, LANES)
        a_imag = a_imag_ref[...].reshape(C, 1, 8, LANES)
        both = jnp.concatenate(
            [s_real * a_real + s_imag * a_imag, s_real * a_imag - s_imag * a_real], 1
        )
        out_ref[c] = both.reshape(C * 2 * 8, LANES).astype(BF16)
        return carry

    lax.fori_loop(0, C, one, 0)


def y_backward_kernel(in_ref, table_ref, out_ref):
    out_ref[...] = dot(table_ref[...], in_ref[...]).astype(BF16)


def point_kernel(field_ref, cotangent_ref, point_ref, point_out, cotangent_out, wide, other):
    wide[...] = field_ref[...].astype(F32)
    other[...] = cotangent_ref[...].astype(F32)
    for y in range(YL):
        point_out[y] = dot(point_ref[...], cells_of(wide, y).astype(BF16))
        cotangent_out[y] = cells_of(other, y).astype(BF16)


def cell_kernel(
    in_ref, point_ref, cotangent_ref, zt_bwd_ref, zt_fwd_ref, out_ref, slope_ref, layer_ref, spread
):
    unpack(in_ref, spread)
    modes = [modes_of(spread, y).astype(BF16) for y in range(YL)]
    for y in range(YL):
        pre = dot(modes[y], zt_bwd_ref[...], 0, 0) + point_ref[y]
        value, slope = gelu_parts(pre)
        layer_ref[y] = value.astype(BF16)
        slope_ref[y] = (cotangent_ref[y].astype(F32) * slope).astype(BF16)
    for y in range(YL):
        put_modes(spread, y, slope_ref[y], zt_fwd_ref[...])
    pack(spread, out_ref)


def after_kernel(slope_ref, layer_ref, point_ref, point_out, layer_out, wide):
    for y in range(YL):
        point_out[y] = dot(point_ref[...], slope_ref[y])
        put_cells(wide, y, layer_ref[y].astype(F32))
    layer_out[...] = wide[...].astype(BF16)


def close_kernel(in_ref, point_ref, zt_bwd_ref, out_ref, spread, wide):
    unpack(in_ref, spread)
    for y in range(YL):
        modes = modes_of(spread, y).astype(BF16)
        put_cells(wide, y, dot(modes, zt_bwd_ref[...], 0, 0) + point_ref[y])
    out_ref[...] = wide[...].astype(BF16)


ROWS = T * C * XL * YL
ZT = (MZ * YL * 2, T * LANES)
AFTER_Y = (GX * XL * 2, 2 * LANES)
AFTER_X = (GX * JL * 2, T * LANES)
ZT_SPREAD = (T, MZ * YL * 2, LANES)
Y_SPREAD = (2, GX * XL * 2, LANES)
X_SPREAD = (T, GX * JL * 2, LANES)
CELLS = (YL, C * XL, T * Z)
PARTS = (C * 8, LANES)


def call(kernel, outs, operands, scratch=(), scalars=(), flops=10**8):
    vmem = pl.BlockSpec(memory_space=pltpu.VMEM)
    smem = pl.BlockSpec(memory_space=pltpu.SMEM)
    single = len(outs) == 1
    specs = [smem if i in scalars else vmem for i in range(len(operands))]
    moved = sum(math.prod(o.shape) * o.dtype.itemsize for o in list(outs) + list(operands))
    return pl.pallas_call(
        kernel,
        out_shape=outs[0] if single else tuple(outs),
        in_specs=specs,
        out_specs=vmem if single else (vmem,) * len(outs),
        scratch_shapes=[pltpu.VMEM(shape, F32) for shape in scratch],
        cost_estimate=pl.CostEstimate(flops=flops, bytes_accessed=moved, transcendentals=0),
        compiler_params=pltpu.CompilerParams(vmem_limit_bytes=24 * 1024 * 1024),
    )(*operands)


def shaped(shape, dtype=BF16):
    return jax.ShapeDtypeStruct(shape, dtype)


def exchange(block, axis):
    return lax.all_to_all(block, axis, split_axis=0, concat_axis=0, tiled=True)


def on_device(grid_field, spectral_weight, point_weight, cotangent):
    zt_fwd, zt_bwd, y_fwd, y_bwd, x_fwd, x_bwd = (jnp.asarray(a) for a in tables())
    field = grid_field.reshape(ROWS, Z)
    cotan = cotangent.reshape(ROWS, Z)
    weight = (
        spectral_weight.reshape(C, C, JL, 4, LANES)
        .transpose(0, 1, 3, 2, 4)
        .reshape(C, C * 2 * 8, LANES)
    )
    eye = jnp.eye(XL, dtype=BF16)
    point_back = jnp.kron(point_weight, eye)
    point_fwd = jnp.kron(point_weight.T, eye)
    kz = lax.axis_index("gy")
    scale = (jnp.where(kz == 0, 1.0, 2.0).astype(F32) / float(X * Y * Z * T)).reshape(1)
    wide = (ROWS, Z)

    opened = call(open_kernel, [shaped(ZT)], [field, zt_fwd], [wide, ZT_SPREAD])
    opened = exchange(opened, "gy")
    point, cotan = call(
        point_kernel,
        [shaped(CELLS, F32), shaped(CELLS)],
        [field, cotan, point_fwd],
        [wide, wide],
    )
    halved = call(y_forward_kernel, [shaped(AFTER_Y)], [opened, y_fwd], [Y_SPREAD])
    halved = exchange(halved, "gx")
    mixed, spec_real, spec_imag = call(
        mix_kernel,
        [shaped(AFTER_X), shaped(PARTS, F32), shaped(PARTS, F32)],
        [halved, weight, scale, x_fwd, x_bwd],
        [X_SPREAD],
        (2,),
    )
    mixed = exchange(mixed, "gx")
    along_y = call(y_backward_kernel, [shaped(ZT)], [mixed, y_bwd])
    along_y = exchange(along_y, "gy")
    turned, slope, layer = call(
        cell_kernel,
        [shaped(ZT), shaped(CELLS), shaped(CELLS)],
        [along_y, point, cotan, zt_bwd, zt_fwd],
        [ZT_SPREAD],
    )
    turned = exchange(turned, "gy")
    point, layer_out = call(
        after_kernel, [shaped(CELLS, F32), shaped(wide)], [slope, layer, point_back], [wide]
    )
    halved = call(y_forward_kernel, [shaped(AFTER_Y)], [turned, y_fwd], [Y_SPREAD])
    halved = exchange(halved, "gx")
    back, adj_real, adj_imag = call(
        back_kernel,
        [shaped(AFTER_X), shaped(PARTS, F32), shaped(PARTS, F32)],
        [halved, weight, scale, x_fwd, x_bwd],
        [PARTS, PARTS, X_SPREAD],
        (2,),
    )
    back = exchange(back, "gx")
    grad_spectral = call(
        grad_kernel,
        [shaped((C, C * 2 * 8, LANES))],
        [spec_real, spec_imag, adj_real, adj_imag, scale],
        (),
        (4,),
    )
    along_y = call(y_backward_kernel, [shaped(ZT)], [back, y_bwd])
    along_y = exchange(along_y, "gy")
    grad_field = call(close_kernel, [shaped(wide)], [along_y, point, zt_bwd], [ZT_SPREAD, wide])

    grad_spectral = (
        grad_spectral.reshape(C, C, 4, JL, LANES)
        .transpose(0, 1, 3, 2, 4)
        .reshape(spectral_weight.shape)
    )
    return (
        layer_out.reshape(grid_field.shape),
        grad_field.reshape(grid_field.shape),
        grad_spectral,
    )


def solution(mesh):
    field = P(None, None, None, "gx", "gy", None)
    modes = P(None, None, "gx", "gy", None)
    return jax.shard_map(
        on_device,
        mesh=mesh,
        in_specs=(field, modes, P(), field),
        out_specs=(field, field, modes),
        check_vma=False,
    )
```

profile of v0, /device:TPU:8, one launch (start us, length us, event | category | flops | bytes accessed | tf_op | source)
XLA Modules:
  0.0 152.8 jit_solution(3486148579568880438)
XLA Ops:
  0.6 0.0 copy-start.1
  0.6 0.9 copy-done.1
  1.6 0.0 copy-start.3
  1.6 1.0 copy-done.3
  2.6 0.5 shard_map.121
  3.1 0.0 copy-start.15
  3.1 25.8 %all_to_all.88 = bf16[32,8,512]{2,1,0:T(8,128)(2,1)S(1)} all-to-all(bf16[32,8,512]{2,1,0:T(8,128)(2,1)S(1)} %bitcast.43), channel_id=1, replica_groups=mesh['gx'=16,'gy'=32] {'gy'}, dimensions={0} | all-to-all | bytes 524288 | tf_op jit(solution)/shard_map/all_to_all | solution.py:366
  28.9 0.0 copy-done.15
  28.9 1.1 shard_map.122
  30.0 0.0 copy-start.13
  30.0 0.0 copy-start.14
  30.0 10.3 %all-to-all-start.1 = ((bf16[16,16,256]{2,1,0:T(8,128)(2,1)}), bf16[16,16,256]{2,1,0:T(8,128)(2,1)S(1)}, u32[]{:S(2)}, u32[]{:S(2)}) async-start(bf16[16,16,256]{2,1,0:T(8,128)(2,1)} %bitcast.3), calls=%async_computation.1 | async-start | bytes 262144 | tf_op jit(solution)/shard_map/all_to_all | solution.py:366
  40.3 10.6 %all-to-all-done.1 = bf16[16,16,256]{2,1,0:T(8,128)(2,1)S(1)} async-done(((bf16[16,16,256]{2,1,0:T(8,128)(2,1)}), bf16[16,16,256]{2,1,0:T(8,128)(2,1)S(1)}, u32[]{:S(2)}, u32[]{:S(2)}) %all-to-all-start.1) | async-done | bytes 131104 | tf_op jit(solution)/shard_map/all_to_all | solution.py:366
  50.9 0.0 copy-done
  50.9 0.0 copy-done.13
  50.9 0.0 copy-done.14
  50.9 1.4 shard_map.123
  52.3 0.0 copy-start.16
  52.3 0.6 copy-done.16
  52.9 0.0 copy-start.12
  52.9 13.3 %all_to_all.89 = bf16[16,8,512]{2,1,0:T(8,128)(2,1)S(1)} all-to-all(bf16[16,8,512]{2,1,0:T(8,128)(2,1)S(1)} %bitcast.53), channel_id=1, replica_groups=mesh['gx'=16,'gy'=32] {'gx'}, dimensions={0} | all-to-all | bytes 262144 | tf_op jit(solution)/shard_map/all_to_all | solution.py:366
  66.3 0.0 copy-done.12
  66.3 0.9 shard_map.124
  67.2 0.0 copy-start.19
  67.2 5.4 %all-to-all-start.3 = ((bf16[32,8,512]{2,1,0:T(8,128)(2,1)}), bf16[32,8,512]{2,1,0:T(8,128)(2,1)S(1)}, u32[]{:S(2)}, u32[]{:S(2)}) async-start(bf16[32,8,512]{2,1,0:T(8,128)(2,1)} %bitcast.11), calls=%async_computation.3 | async-start | bytes 524288 | tf_op jit(solution)/shard_map/all_to_all | solution.py:366
  72.6 0.0 copy-done.19
  72.6 0.1 copy.17
  72.7 0.9 broadcast_multiply_fusion
  73.6 0.0 copy-start.4
  73.6 0.5 mul.44.point_ref
  74.1 0.5 copy-done.4
  74.6 0.0 copy-start.5
  74.6 1.0 copy-done.5
  75.7 0.0 copy-start.2
  75.7 0.5 shard_map.125
  76.2 0.0 copy-start.10
  76.2 0.8 copy-done.10
  77.0 8.2 %all-to-all-done.3 = bf16[32,8,512]{2,1,0:T(8,128)(2,1)S(1)} async-done(((bf16[32,8,512]{2,1,0:T(8,128)(2,1)}), bf16[32,8,512]{2,1,0:T(8,128)(2,1)S(1)}, u32[]{:S(2)}, u32[]{:S(2)}) %all-to-all-start.3) | async-done | bytes 262176 | tf_op jit(solution)/shard_map/all_to_all | solution.py:366
  85.2 0.0 copy-done.2
  85.2 0.0 copy-start.11
  85.2 1.0 copy-done.11
  86.2 1.3 shard_map.126
  87.6 0.0 copy-start.6
  87.6 0.0 copy-start.8
  87.6 16.4 %all_to_all.90 = bf16[32,8,512]{2,1,0:T(8,128)(2,1)S(1)} all-to-all(bf16[32,8,512]{2,1,0:T(8,128)(2,1)S(1)} %bitcast.51), channel_id=1, replica_groups=mesh['gx'=16,'gy'=32] {'gy'}, dimensions={0} | all-to-all | bytes 524288 | tf_op jit(solution)/shard_map/all_to_all | solution.py:366
  104.0 0.5 shard_map.128
  104.4 13.5 %all_to_all.91 = bf16[16,16,256]{2,1,0:T(8,128)(2,1)S(1)} all-to-all(bf16[16,16,256]{2,1,0:T(8,128)(2,1)S(1)} %bitcast.47), channel_id=1, replica_groups=mesh['gx'=16,'gy'=32] {'gx'}, dimensions={0} | all-to-all | bytes 262144 | tf_op jit(solution)/shard_map/all_to_all | solution.py:366
  117.9 0.0 copy-done.6
  117.9 0.0 copy-done.8
  117.9 1.3 shard_map.129
  119.2 0.0 copy-start.18
  119.3 13.3 %all_to_all.92 = bf16[16,8,512]{2,1,0:T(8,128)(2,1)S(1)} all-to-all(bf16[16,8,512]{2,1,0:T(8,128)(2,1)S(1)} %bitcast.52), channel_id=1, replica_groups=mesh['gx'=16,'gy'=32] {'gx'}, dimensions={0} | all-to-all | bytes 262144 | tf_op jit(solution)/shard_map/all_to_all | solution.py:366
  132.6 0.9 shard_map.130
  133.5 5.4 %all-to-all-start.7 = ((bf16[32,8,512]{2,1,0:T(8,128)(2,1)}), bf16[32,8,512]{2,1,0:T(8,128)(2,1)S(1)}, u32[]{:S(2)}, u32[]{:S(2)}) async-start(bf16[32,8,512]{2,1,0:T(8,128)(2,1)} %bitcast.24), calls=%async_computation.7 | async-start | bytes 524288 | tf_op jit(solution)/shard_map/all_to_all | solution.py:366
  138.9 0.0 copy-done.18
  138.9 0.5 mul.47.point_ref
  139.4 0.0 copy-done.7
  139.4 0.0 copy-done.9
  139.4 0.0 copy-start.17
  139.4 1.2 shard_map.127
  140.6 0.0 copy-done.17
  140.6 1.3 shard_map.132
  142.0 9.6 %all-to-all-done.7 = bf16[32,8,512]{2,1,0:T(8,128)(2,1)S(1)} async-done(((bf16[32,8,512]{2,1,0:T(8,128)(2,1)}), bf16[32,8,512]{2,1,0:T(8,128)(2,1)S(1)}, u32[]{:S(2)}, u32[]{:S(2)}) %all-to-all-start.7) | async-done | bytes 262176 | tf_op jit(solution)/shard_map/all_to_all | solution.py:366
  151.5 1.2 shard_map.131
  (4 shorter events, 0.0 us)
Async XLA Ops:
  0.6 1.0 copy-start.1
  1.6 1.0 copy-start.3
  2.6 48.3 %copy-start = (bf16[16,16,4,1,512]{4,2,3,1,0:T(4,128)(2,1)S(1)}, bf16[16,16,4,1,512]{4,2,3,1,0:T(4,128)(2,1)}, u32[]{:S(2)}) copy-start(bf16[16,16,4,1,512]{4,2,3,1,0:T(4,128)(2,1)} %param.11) | copy-start | bytes 3145732
  3.1 25.8 %copy-start.15 = (bf16[128,256]{1,0:T(8,128)(2,1)S(1)}, bf16[128,256]{1,0:T(8,128)(2,1)}, u32[]{:S(2)}) copy-start(bf16[128,256]{1,0:T(8,128)(2,1)} %constant.24.clone.table_ref) | copy-start | bytes 196612
  30.0 20.9 %copy-start.13 = (bf16[256,128]{1,0:T(8,128)(2,1)S(1)}, bf16[256,128]{1,0:T(8,128)(2,1)}, u32[]{:S(2)}) copy-start(bf16[256,128]{1,0:T(8,128)(2,1)} %constant.27.clone.x_bwd_ref) | copy-start | bytes 196612
  30.0 20.9 %copy-start.14 = (bf16[256,128]{1,0:T(8,128)(2,1)S(1)}, bf16[256,128]{1,0:T(8,128)(2,1)}, u32[]{:S(2)}) copy-start(bf16[256,128]{1,0:T(8,128)(2,1)} %constant.26.clone.x_fwd_ref) | copy-start | bytes 196612
  30.0 20.9 %all-to-all-start.1 = ((bf16[16,16,256]{2,1,0:T(8,128)(2,1)}), bf16[16,16,256]{2,1,0:T(8,128)(2,1)S(1)}, u32[]{:S(2)}, u32[]{:S(2)}) async-start(bf16[16,16,256]{2,1,0:T(8,128)(2,1)} %bitcast.3), calls=%async_computation.1 | async-start | bytes 262144 | tf_op jit(solution)/shard_map/all_to_all | solution.py:366
  52.3 0.6 copy-start.16
  52.9 13.3 %copy-start.12 = (bf16[256,128]{1,0:T(8,128)(2,1)S(1)}, bf16[256,128]{1,0:T(8,128)(2,1)}, u32[]{:S(2)}) copy-start(bf16[256,128]{1,0:T(8,128)(2,1)} %constant.25.clone.table_ref) | copy-start | bytes 196612
  67.2 5.4 %copy-start.19 = (bf16[16,16]{1,0:T(8,128)(2,1)S(1)}, bf16[16,16]{1,0:T(8,128)(2,1)}, u32[]{:S(2)}) copy-start(bf16[16,16]{1,0:T(8,128)(2,1)} %param.12) | copy-start | bytes 1540
  67.2 18.0 %all-to-all-start.3 = ((bf16[32,8,512]{2,1,0:T(8,128)(2,1)}), bf16[32,8,512]{2,1,0:T(8,128)(2,1)S(1)}, u32[]{:S(2)}, u32[]{:S(2)}) async-start(bf16[32,8,512]{2,1,0:T(8,128)(2,1)} %bitcast.11), calls=%async_computation.3 | async-start | bytes 524288 | tf_op jit(solution)/shard_map/all_to_all | solution.py:366
  73.6 1.0 copy-start.4
  74.6 1.0 copy-start.5
  75.7 9.5 %copy-start.2 = (bf16[256,512]{1,0:T(8,128)(2,1)S(1)}, bf16[256,512]{1,0:T(8,128)(2,1)}, u32[]{:S(2)}) copy-start(bf16[256,512]{1,0:T(8,128)(2,1)} %constant.23.clone.zt_ref.zt_bwd_ref.zt_fwd_ref) | copy-start | bytes 786436
  76.2 0.8 copy-start.10
  85.2 1.0 copy-start.11
  87.6 30.3 %copy-start.6 = (bf16[4,128,512]{2,1,0:T(8,128)(2,1)}, bf16[4,128,512]{2,1,0:T(8,128)(2,1)S(1)}, u32[]{:S(2)}) copy-start(bf16[4,128,512]{2,1,0:T(8,128)(2,1)S(1)} %get-tuple-element.19.slope_ref) | copy-start | bytes 1572868
  87.6 30.3 %copy-start.8 = (bf16[4,128,512]{2,1,0:T(8,128)(2,1)}, bf16[4,128,512]{2,1,0:T(8,128)(2,1)S(1)}, u32[]{:S(2)}) copy-start(bf16[4,128,512]{2,1,0:T(8,128)(2,1)S(1)} %get-tuple-element.20.layer_ref) | copy-start | bytes 1572868
  119.2 19.7 %copy-start.18 = (bf16[16,8,16,8]{3,2,1,0:T(8,128)(2,1)S(1)}, bf16[16,8,16,8]{3,2,1,0:T(8,128)(2,1)}, u32[]{:S(2)}) copy-start(bf16[16,8,16,8]{3,2,1,0:T(8,128)(2,1)} %get-tuple-element.29) | copy-start | bytes 98308
  133.5 5.9 %copy-start.7 = (bf16[4,128,512]{2,1,0:T(8,128)(2,1)S(1)}, bf16[4,128,512]{2,1,0:T(8,128)(2,1)}, u32[]{:S(2)}) copy-start(bf16[4,128,512]{2,1,0:T(8,128)(2,1)} %copy-done.6) | copy-start | bytes 1572868
  133.5 5.9 %copy-start.9 = (bf16[4,128,512]{2,1,0:T(8,128)(2,1)S(1)}, bf16[4,128,512]{2,1,0:T(8,128)(2,1)}, u32[]{:S(2)}) copy-start(bf16[4,128,512]{2,1,0:T(8,128)(2,1)} %copy-done.8) | copy-start | bytes 1572868
  133.5 18.0 %all-to-all-start.7 = ((bf16[32,8,512]{2,1,0:T(8,128)(2,1)}), bf16[32,8,512]{2,1,0:T(8,128)(2,1)S(1)}, u32[]{:S(2)}, u32[]{:S(2)}) async-start(bf16[32,8,512]{2,1,0:T(8,128)(2,1)} %bitcast.24), calls=%async_computation.7 | async-start | bytes 524288 | tf_op jit(solution)/shard_map/all_to_all | solution.py:366
  139.4 1.2 copy-start.17
where the time goes:
time: 154 us; the launch traced here: 153 us
  blocking collectives  82.3 us (53%)
  waiting for transfers between devices  28.3 us (18%)
  starting transfers between devices  21 us (14%)
  Pallas kernels  12.2 us (8%)
  local copies, waits for them, and re-layouts  7.14 us (5%)
    all_to_all x5, blocking collectives, exchange(): return lax.all_to_all(block, axis, split_axis=0, concat_axis=0, tiled=True)  82.3 us
    all_to_all x3, waiting for transfers between devices, exchange(): return lax.all_to_all(block, axis, split_axis=0, concat_axis=0, tiled=True)  28.3 us
    all_to_all x3, starting transfers between devices, exchange(): return lax.all_to_all(block, axis, split_axis=0, concat_axis=0, tiled=True)  21 us
    pallas_call x12, Pallas kernels, call(): pl.pallas_call(kernel, out_shape=outs[0] if single else tuple(outs), in_s...  12.2 us
    unnamed x40, local copies, waits for them, and re-layouts  6.07 us
  transfers between devices with their start and end apart: 3, of which 3 were waited for; matrix products, arithmetic and copies ran while one was open for 1% of the time, Pallas kernels for 2%

commit v1 on v0

--- a/solution.py
+++ b/solution.py
@@ -22,6 +22,7 @@
 YL = Y // GY
 JL = MY // GX
 LANES = 128
+GY_ORDER = [y * 4 + z for y in (0, 4, 2, 6, 1, 5, 3, 7) for z in range(4)]
 
 F32 = jnp.float32
 BF16 = jnp.bfloat16
@@ -46,6 +47,7 @@
     quarter = np.mod(np.arange(T)[:, None] * np.arange(T)[None, :], T)
     ct = np.array([1.0, 0.0, -1.0, 0.0])[quarter]
     st = np.array([0.0, 1.0, 0.0, -1.0])[quarter]
+    cz, sz = cz[GY_ORDER], sz[GY_ORDER]
     both_cos = (
         cz[None, :, None, :] * ct[:, None, :, None] - sz[None, :, None, :] * st[:, None, :, None]
     )
@@ -61,13 +63,14 @@
     fwd[:, 0, :, 1] = sy
     fwd[:, 1, :, 0] = -sy
     fwd[:, 1, :, 1] = cy
+    fwd = fwd.reshape(MY * 2, GY, YL * 2)[:, GY_ORDER]
     y_fwd = fwd.reshape(GX, JL, 2, Y * 2).transpose(1, 2, 0, 3).reshape(MY * 2, Y * 2)
     bwd = np.empty((Y, 2, MY, 2))
     bwd[:, 0, :, 0] = cy.T
     bwd[:, 0, :, 1] = -sy.T
     bwd[:, 1, :, 0] = sy.T
     bwd[:, 1, :, 1] = cy.T
-    y_bwd = bwd.reshape(Y * 2, MY * 2)
+    y_bwd = bwd.reshape(GY, YL * 2, MY * 2)[GY_ORDER].reshape(Y * 2, MY * 2)
 
     cx, sx = (a.astype(np.float64) for a in cos_sin(signed(MX), X))
     fwd = np.empty((X, 2, 2, MX))
@@ -158,10 +161,20 @@
     )
 
 
-def open_kernel(field_ref, zt_ref, out_ref, wide, spread):
-    wide[...] = field_ref[...].astype(F32)
+def open_kernel(field_hbm, zt_hbm, out_ref, field, zt_fwd, wide, spread, sems):
+    rows = C * XL * YL
+    copies = [pltpu.make_async_copy(zt_hbm, zt_fwd, sems.at[T])]
+    for t in range(T):
+        part = pl.ds(t * rows, rows)
+        copies.append(pltpu.make_async_copy(field_hbm.at[part], field.at[part], sems.at[t]))
+    for copy in copies:
+        copy.start()
+    for t in range(T):
+        copies[1 + t].wait()
+        wide[t * rows : (t + 1) * rows] = field[t * rows : (t + 1) * rows].astype(F32)
+    copies[0].wait()
     for y in range(YL):
-        put_modes(spread, y, cells_of(wide, y).astype(BF16), zt_ref[...])
+        put_modes(spread, y, cells_of(wide, y).astype(BF16), zt_fwd[...])
     pack(spread, out_ref)
 
 
@@ -248,16 +261,36 @@
     scale_ref,
     x_fwd_ref,
     x_bwd_ref,
+    s_real_ref,
+    s_imag_ref,
     out_ref,
+    grad_hbm,
     real_ref,
     imag_ref,
     back_real,
     back_imag,
     spread,
+    grad,
+    sem,
 ):
     real, imag = to_spectrum(in_ref, x_fwd_ref)
     real_ref[...] = real
     imag_ref[...] = imag
+
+    def outer(c, carry):
+        s_real = (at_channel(s_real_ref, c).astype(F32) * scale_ref[0])[None, None]
+        s_imag = (at_channel(s_imag_ref, c).astype(F32) * scale_ref[0])[None, None]
+        a_real = real_ref[...].reshape(C, 1, 8, LANES)
+        a_imag = imag_ref[...].reshape(C, 1, 8, LANES)
+        both = jnp.concatenate(
+            [s_real * a_real + s_imag * a_imag, s_real * a_imag - s_imag * a_real], 1
+        )
+        grad[c] = both.reshape(C * 2 * 8, LANES).astype(BF16)
+        return carry
+
+    lax.fori_loop(0, C, outer, 0)
+    send = pltpu.make_async_copy(grad, grad_hbm, sem)
+    send.start()
 
     def one(c, carry):
         a_real = real_ref[...].reshape(C, 8, LANES)
@@ -271,62 +304,74 @@
     lax.fori_loop(0, C, one, 0)
     scale = scale_ref[0]
     from_spectrum(back_real[...] * scale, back_imag[...] * scale, x_bwd_ref, out_ref, spread)
-
-
-def grad_kernel(s_real_ref, s_imag_ref, a_real_ref, a_imag_ref, scale_ref, out_ref):
-    def one(c, carry):
-        s_real = (at_channel(s_real_ref, c) * scale_ref[0])[None]
-        s_imag = (at_channel(s_imag_ref, c) * scale_ref[0])[None]
-        a_real = a_real_ref[...].reshape(C, 1, 8, LANES)
-        a_imag = a_imag_ref[...].reshape(C, 1, 8, LANES)
-        both = jnp.concatenate(
-            [s_real * a_real + s_imag * a_imag, s_real * a_imag - s_imag * a_real], 1
-        )
-        out_ref[c] = both.reshape(C * 2 * 8, LANES).astype(BF16)
-        return carry
-
-    lax.fori_loop(0, C, one, 0)
+    send.wait()
 
 
 def y_backward_kernel(in_ref, table_ref, out_ref):
     out_ref[...] = dot(table_ref[...], in_ref[...]).astype(BF16)
 
 
-def point_kernel(field_ref, cotangent_ref, point_ref, point_out, cotangent_out, wide, other):
-    wide[...] = field_ref[...].astype(F32)
-    other[...] = cotangent_ref[...].astype(F32)
-    for y in range(YL):
-        point_out[y] = dot(point_ref[...], cells_of(wide, y).astype(BF16))
-        cotangent_out[y] = cells_of(other, y).astype(BF16)
+def point_table(point_ref, back):
+    shape = (C * XL, C)
+    row = lax.broadcasted_iota(jnp.int32, shape, 0)
+    pick = (row // XL == lax.broadcasted_iota(jnp.int32, shape, 1)).astype(F32).astype(BF16)
+    half = dot(pick, point_ref[...], 1, 0 if back else 1).astype(BF16)
+    full = dot(half, pick, 1, 1)
+    row = lax.broadcasted_iota(jnp.int32, full.shape, 0)
+    column = lax.broadcasted_iota(jnp.int32, full.shape, 1)
+    return jnp.where(row % XL == column % XL, full, 0.0).astype(BF16)
 
 
 def cell_kernel(
-    in_ref, point_ref, cotangent_ref, zt_bwd_ref, zt_fwd_ref, out_ref, slope_ref, layer_ref, spread
+    in_ref,
+    field_hbm,
+    cotangent_hbm,
+    point_ref,
+    zt_bwd_ref,
+    zt_fwd_ref,
+    out_ref,
+    slope_ref,
+    layer_hbm,
+    field,
+    cotangent,
+    wide,
+    other,
+    spread,
+    sems,
 ):
+    copies = [
+        pltpu.make_async_copy(field_hbm, field, sems.at[0]),
+        pltpu.make_async_copy(cotangent_hbm, cotangent, sems.at[1]),
+    ]
+    for copy in copies:
+        copy.start()
+    point = point_table(point_ref, False)
     unpack(in_ref, spread)
     modes = [modes_of(spread, y).astype(BF16) for y in range(YL)]
+    copies[0].wait()
+    wide[...] = field[...].astype(F32)
+    copies[1].wait()
+    other[...] = cotangent[...].astype(F32)
     for y in range(YL):
-        pre = dot(modes[y], zt_bwd_ref[...], 0, 0) + point_ref[y]
+        pre = dot(modes[y], zt_bwd_ref[...], 0, 0) + dot(point, cells_of(wide, y).astype(BF16))
         value, slope = gelu_parts(pre)
-        layer_ref[y] = value.astype(BF16)
-        slope_ref[y] = (cotangent_ref[y].astype(F32) * slope).astype(BF16)
+        put_cells(wide, y, value)
+        slope_ref[y] = (cells_of(other, y) * slope).astype(BF16)
+    field[...] = wide[...].astype(BF16)
+    send = pltpu.make_async_copy(field, layer_hbm, sems.at[2])
+    send.start()
     for y in range(YL):
         put_modes(spread, y, slope_ref[y], zt_fwd_ref[...])
     pack(spread, out_ref)
-
-
-def after_kernel(slope_ref, layer_ref, point_ref, point_out, layer_out, wide):
-    for y in range(YL):
-        point_out[y] = dot(point_ref[...], slope_ref[y])
-        put_cells(wide, y, layer_ref[y].astype(F32))
-    layer_out[...] = wide[...].astype(BF16)
-
-
-def close_kernel(in_ref, point_ref, zt_bwd_ref, out_ref, spread, wide):
+    send.wait()
+
+
+def close_kernel(in_ref, slope_ref, point_ref, zt_bwd_ref, out_ref, spread, wide):
+    point = point_table(point_ref, True)
     unpack(in_ref, spread)
     for y in range(YL):
         modes = modes_of(spread, y).astype(BF16)
-        put_cells(wide, y, dot(modes, zt_bwd_ref[...], 0, 0) + point_ref[y])
+        put_cells(wide, y, dot(modes, zt_bwd_ref[...], 0, 0) + dot(point, slope_ref[y]))
     out_ref[...] = wide[...].astype(BF16)
 
 
@@ -341,20 +386,32 @@
 PARTS = (C * 8, LANES)
 
 
-def call(kernel, outs, operands, scratch=(), scalars=(), flops=10**8):
-    vmem = pl.BlockSpec(memory_space=pltpu.VMEM)
+WIDE = (ROWS, Z)
+GRAD = (C, C * 2 * 8, LANES)
+
+
+def vmem(shape, dtype=F32):
+    return pltpu.VMEM(shape, dtype)
+
+
+def call(kernel, outs, operands, scratch=(), scalars=(), far=(), far_outs=(), flops=10**8):
+    near = pl.BlockSpec(memory_space=pltpu.VMEM)
     smem = pl.BlockSpec(memory_space=pltpu.SMEM)
+    anywhere = pl.BlockSpec(memory_space=pltpu.HBM)
+    specs = [
+        smem if i in scalars else anywhere if i in far else near for i in range(len(operands))
+    ]
+    out_specs = tuple(anywhere if i in far_outs else near for i in range(len(outs)))
     single = len(outs) == 1
-    specs = [smem if i in scalars else vmem for i in range(len(operands))]
     moved = sum(math.prod(o.shape) * o.dtype.itemsize for o in list(outs) + list(operands))
     return pl.pallas_call(
         kernel,
         out_shape=outs[0] if single else tuple(outs),
         in_specs=specs,
-        out_specs=vmem if single else (vmem,) * len(outs),
-        scratch_shapes=[pltpu.VMEM(shape, F32) for shape in scratch],
+        out_specs=out_specs[0] if single else out_specs,
+        scratch_shapes=list(scratch),
         cost_estimate=pl.CostEstimate(flops=flops, bytes_accessed=moved, transcendentals=0),
-        compiler_params=pltpu.CompilerParams(vmem_limit_bytes=24 * 1024 * 1024),
+        compiler_params=pltpu.CompilerParams(vmem_limit_bytes=16 * 1024 * 1024),
     )(*operands)
 
 
@@ -363,75 +420,92 @@
 
 
 def exchange(block, axis):
-    return lax.all_to_all(block, axis, split_axis=0, concat_axis=0, tiled=True)
+    groups = [GY_ORDER] if axis == "gy" else None
+    return lax.all_to_all(
+        block, axis, split_axis=0, concat_axis=0, axis_index_groups=groups, tiled=True
+    )
+
+
+def open_stage(field, zt_fwd):
+    scratch = [vmem(WIDE, BF16), vmem(ZT, BF16), vmem(WIDE), vmem(ZT_SPREAD)]
+    scratch.append(pltpu.SemaphoreType.DMA((T + 1,)))
+    return call(open_kernel, [shaped(ZT)], [field, zt_fwd], scratch, far=(0, 1))
+
+
+def y_forward_stage(block, y_fwd):
+    return call(y_forward_kernel, [shaped(AFTER_Y)], [block, y_fwd], [vmem(Y_SPREAD)])
+
+
+def mix_stage(block, weight, scale, x_fwd, x_bwd):
+    return call(
+        mix_kernel,
+        [shaped(AFTER_X), shaped(PARTS, F32), shaped(PARTS, F32)],
+        [block, weight, scale, x_fwd, x_bwd],
+        [vmem(X_SPREAD)],
+        scalars=(2,),
+    )
+
+
+def y_backward_stage(block, y_bwd):
+    return call(y_backward_kernel, [shaped(ZT)], [block, y_bwd])
+
+
+def cell_stage(block, field, cotangent, point_weight, zt_bwd, zt_fwd):
+    scratch = [vmem(WIDE, BF16), vmem(WIDE, BF16), vmem(WIDE), vmem(WIDE), vmem(ZT_SPREAD)]
+    scratch.append(pltpu.SemaphoreType.DMA((3,)))
+    return call(
+        cell_kernel,
+        [shaped(ZT), shaped(CELLS), shaped(WIDE)],
+        [block, field, cotangent, point_weight, zt_bwd, zt_fwd],
+        scratch,
+        far=(1, 2),
+        far_outs=(2,),
+    )
+
+
+def back_stage(block, weight, scale, x_fwd, x_bwd, spec_real, spec_imag):
+    scratch = [vmem(PARTS)] * 4 + [vmem(X_SPREAD), vmem(GRAD, BF16), pltpu.SemaphoreType.DMA]
+    return call(
+        back_kernel,
+        [shaped(AFTER_X), shaped(GRAD)],
+        [block, weight, scale, x_fwd, x_bwd, spec_real, spec_imag],
+        scratch,
+        scalars=(2,),
+        far_outs=(1,),
+    )
+
+
+def close_stage(block, slope, point_weight, zt_bwd):
+    return call(
+        close_kernel,
+        [shaped(WIDE)],
+        [block, slope, point_weight, zt_bwd],
+        [vmem(ZT_SPREAD), vmem(WIDE)],
+    )
 
 
 def on_device(grid_field, spectral_weight, point_weight, cotangent):
     zt_fwd, zt_bwd, y_fwd, y_bwd, x_fwd, x_bwd = (jnp.asarray(a) for a in tables())
-    field = grid_field.reshape(ROWS, Z)
-    cotan = cotangent.reshape(ROWS, Z)
-    weight = (
-        spectral_weight.reshape(C, C, JL, 4, LANES)
-        .transpose(0, 1, 3, 2, 4)
-        .reshape(C, C * 2 * 8, LANES)
-    )
-    eye = jnp.eye(XL, dtype=BF16)
-    point_back = jnp.kron(point_weight, eye)
-    point_fwd = jnp.kron(point_weight.T, eye)
+    field = grid_field.reshape(WIDE)
+    cotan = cotangent.reshape(WIDE)
+    weight = spectral_weight.reshape(C, C, JL, 4, LANES).transpose(0, 1, 3, 2, 4).reshape(GRAD)
     kz = lax.axis_index("gy")
     scale = (jnp.where(kz == 0, 1.0, 2.0).astype(F32) / float(X * Y * Z * T)).reshape(1)
-    wide = (ROWS, Z)
-
-    opened = call(open_kernel, [shaped(ZT)], [field, zt_fwd], [wide, ZT_SPREAD])
-    opened = exchange(opened, "gy")
-    point, cotan = call(
-        point_kernel,
-        [shaped(CELLS, F32), shaped(CELLS)],
-        [field, cotan, point_fwd],
-        [wide, wide],
-    )
-    halved = call(y_forward_kernel, [shaped(AFTER_Y)], [opened, y_fwd], [Y_SPREAD])
-    halved = exchange(halved, "gx")
-    mixed, spec_real, spec_imag = call(
-        mix_kernel,
-        [shaped(AFTER_X), shaped(PARTS, F32), shaped(PARTS, F32)],
-        [halved, weight, scale, x_fwd, x_bwd],
-        [X_SPREAD],
-        (2,),
-    )
-    mixed = exchange(mixed, "gx")
-    along_y = call(y_backward_kernel, [shaped(ZT)], [mixed, y_bwd])
-    along_y = exchange(along_y, "gy")
-    turned, slope, layer = call(
-        cell_kernel,
-        [shaped(ZT), shaped(CELLS), shaped(CELLS)],
-        [along_y, point, cotan, zt_bwd, zt_fwd],
-        [ZT_SPREAD],
-    )
-    turned = exchange(turned, "gy")
-    point, layer_out = call(
-        after_kernel, [shaped(CELLS, F32), shaped(wide)], [slope, layer, point_back], [wide]
-    )
-    halved = call(y_forward_kernel, [shaped(AFTER_Y)], [turned, y_fwd], [Y_SPREAD])
-    halved = exchange(halved, "gx")
-    back, adj_real, adj_imag = call(
-        back_kernel,
-        [shaped(AFTER_X), shaped(PARTS, F32), shaped(PARTS, F32)],
-        [halved, weight, scale, x_fwd, x_bwd],
-        [PARTS, PARTS, X_SPREAD],
-        (2,),
-    )
-    back = exchange(back, "gx")
-    grad_spectral = call(
-        grad_kernel,
-        [shaped((C, C * 2 * 8, LANES))],
-        [spec_real, spec_imag, adj_real, adj_imag, scale],
-        (),
-        (4,),
-    )
-    along_y = call(y_backward_kernel, [shaped(ZT)], [back, y_bwd])
-    along_y = exchange(along_y, "gy")
-    grad_field = call(close_kernel, [shaped(wide)], [along_y, point, zt_bwd], [ZT_SPREAD, wide])
+
+    opened = open_stage(field, zt_fwd)
+    opened, scale = lax.optimization_barrier((opened, scale))
+    halved = y_forward_stage(exchange(opened, "gy"), y_fwd)
+    mixed, spec_real, spec_imag = mix_stage(exchange(halved, "gx"), weight, scale, x_fwd, x_bwd)
+    along_y = y_backward_stage(exchange(mixed, "gx"), y_bwd)
+    turned, slope, layer_out = cell_stage(
+        exchange(along_y, "gy"), field, cotan, point_weight, zt_bwd, zt_fwd
+    )
+    halved = y_forward_stage(exchange(turned, "gy"), y_fwd)
+    back, grad_spectral = back_stage(
+        exchange(halved, "gx"), weight, scale, x_fwd, x_bwd, spec_real, spec_imag
+    )
+    along_y = y_backward_stage(exchange(back, "gx"), y_bwd)
+    grad_field = close_stage(exchange(along_y, "gy"), slope, point_weight, zt_bwd)
 
     grad_spectral = (
         grad_spectral.reshape(C, C, 4, JL, LANES)

time: 154 us -> 152 us (0.987)
  blocking collectives: 82.3 us -> 139 us
  waiting for transfers between devices: 28.3 us -> 0 us
  starting transfers between devices: 21 us -> 0 us
  local copies, waits for them, and re-layouts: 7.14 us -> 2.04 us
  Pallas kernels: 12.2 us -> 9.69 us
    all_to_all x5 -> x8, blocking collectives: 82.3 us -> 139 us  [exchange(): lax.all_to_all(block, axis, split_axis=0, concat_axis=0, axis_index_group...]
    all_to_all x3 -> x0, waiting for transfers between devices: 28.3 us -> none  [exchange(): return lax.all_to_all(block, axis, split_axis=0, concat_axis=0, tiled=True)]
    all_to_all x3 -> x0, starting transfers between devices: 21 us -> none  [exchange(): return lax.all_to_all(block, axis, split_axis=0, concat_axis=0, tiled=True)]
    unnamed x40 -> x22, local copies, waits for them, and re-layouts: 6.07 us -> 2.04 us
    pallas_call x12 -> x9, Pallas kernels: 12.2 us -> 9.69 us  [call(): pl.pallas_call(kernel, out_shape=outs[0] if single else tuple(outs), in_s...]
  transfers between devices with their start and end apart: 3 -> 0, of which waited for: 3 -> 0; matrix products, arithmetic and copies ran while one was open for 1% -> 0% of each run, Pallas kernels for 2% -> 0%
where the time goes in v1:
time: 152 us; the launch traced here: 151 us
  blocking collectives  139 us (91%)
  Pallas kernels  9.69 us (6%)
  local copies, waits for them, and re-layouts  2.04 us (1%)
    all_to_all x8, blocking collectives, exchange(): lax.all_to_all(block, axis, split_axis=0, concat_axis=0, axis_index_group...  139 us
    pallas_call x9, Pallas kernels, call(): pl.pallas_call(kernel, out_shape=outs[0] if single else tuple(outs), in_s...  9.69 us

profile of v1, /device:TPU:8, one launch (start us, length us, event | category | flops | bytes accessed | tf_op | source)
XLA Modules:
  0.0 151.1 jit_solution(8317272942050952589)
XLA Ops:
  0.6 0.0 copy-start.1
  0.7 0.9 copy-done.1
  1.6 0.0 copy-start.3
  1.6 1.0 copy-done.3
  2.6 0.0 copy-start
  2.6 1.3 shard_map.121
  3.9 0.0 copy-start.7
  3.9 24.6 %all_to_all.88 = bf16[32,8,512]{2,1,0:T(8,128)(2,1)S(1)} all-to-all(bf16[32,8,512]{2,1,0:T(8,128)(2,1)S(1)} %bitcast.41), channel_id=1, replica_groups={{0,1,2,3,16,17,18,19,8,9,10,11,24,25,26,27,4,5,6,7,20,21,22,23,12,13,14..., dimensions={0} | all-to-all | bytes 524288 | tf_op jit(solution)/shard_map/all_to_all | solution.py:424
  28.6 0.0 copy-done.7
  28.6 0.5 shard_map.122
  29.0 0.0 copy-start.8
  29.1 0.0 copy-start.9
  29.1 20.7 %all_to_all.89 = bf16[16,16,256]{2,1,0:T(8,128)(2,1)S(1)} all-to-all(bf16[16,16,256]{2,1,0:T(8,128)(2,1)S(1)} %bitcast.46), channel_id=1, replica_groups=mesh['gx'=16,'gy'=32] {'gx'}, dimensions={0} | all-to-all | bytes 262144 | tf_op jit(solution)/shard_map/all_to_all | solution.py:424
  49.8 0.0 copy-done
  49.8 0.0 copy-done.8
  49.8 0.0 copy-done.9
  49.8 0.0 copy-start.6
  49.8 1.4 shard_map.123
  51.2 0.0 copy-start.5
  51.2 13.3 %all_to_all.90 = bf16[16,8,512]{2,1,0:T(8,128)(2,1)S(1)} all-to-all(bf16[16,8,512]{2,1,0:T(8,128)(2,1)S(1)} %bitcast.51), channel_id=1, replica_groups=mesh['gx'=16,'gy'=32] {'gx'}, dimensions={0} | all-to-all | bytes 262144 | tf_op jit(solution)/shard_map/all_to_all | solution.py:424
  64.5 0.0 copy-start.4
  64.5 0.0 copy-done.6
  64.5 0.2 shard_map.124
  64.8 0.0 copy-start.10
  64.8 18.7 %all_to_all.91 = bf16[32,8,512]{2,1,0:T(8,128)(2,1)S(1)} all-to-all(bf16[32,8,512]{2,1,0:T(8,128)(2,1)S(1)} %bitcast.39), channel_id=1, replica_groups={{0,1,2,3,16,17,18,19,8,9,10,11,24,25,26,27,4,5,6,7,20,21,22,23,12,13,14..., dimensions={0} | all-to-all | bytes 524288 | tf_op jit(solution)/shard_map/all_to_all | solution.py:424
  83.5 0.0 copy-done.5
  83.5 0.0 copy-done.4
  83.5 0.0 copy-done.10
  83.5 2.4 %shard_map.125 = (bf16[256,512]{1,0:T(8,128)(2,1)S(1)}, bf16[4,128,512]{2,1,0:T(8,128)(2,1)S(1)}, bf16[2048,128]{1,0:T(8,128)(2,1)}) custom-call(bf16[256,512]{1,0:T(8,128)(2,1)S(1)} %bitcast.35, bf16[2048,128]{1,0:T(8,128)(2,1)S(1)} %bitcast.34, bf16[2048,128]{1,0:T(8,128)(2,1)S(1)} %bitcast.42, bf16[16,16]{1,0:T(8,128)(2,1)S(1)} %copy-done.10, ...), custom_call_target="tpu_custom_call" | custom-call | flops 100000000 | bytes 3146240 | tf_op jit(solution)/shard_map/pallas_call | solution.py:407
  85.9 15.8 %all_to_all.92 = bf16[32,8,512]{2,1,0:T(8,128)(2,1)S(1)} all-to-all(bf16[32,8,512]{2,1,0:T(8,128)(2,1)S(1)} %bitcast.49), channel_id=1, replica_groups={{0,1,2,3,16,17,18,19,8,9,10,11,24,25,26,27,4,5,6,7,20,21,22,23,12,13,14..., dimensions={0} | all-to-all | bytes 524288 | tf_op jit(solution)/shard_map/all_to_all | solution.py:424
  101.8 0.5 shard_map.126
  102.2 13.5 %all_to_all.93 = bf16[16,16,256]{2,1,0:T(8,128)(2,1)S(1)} all-to-all(bf16[16,16,256]{2,1,0:T(8,128)(2,1)S(1)} %bitcast.44), channel_id=1, replica_groups=mesh['gx'=16,'gy'=32] {'gx'}, dimensions={0} | all-to-all | bytes 262144 | tf_op jit(solution)/shard_map/all_to_all | solution.py:424
  115.7 1.7 %shard_map.127 = (bf16[128,512]{1,0:T(8,128)(2,1)S(1)}, bf16[16,256,128]{2,1,0:T(8,128)(2,1)}) custom-call(bf16[256,256]{1,0:T(8,128)(2,1)S(1)} %bitcast.48, bf16[16,256,128]{2,1,0:T(8,128)(2,1)S(1)} %bitcast.32, f32[1]{0:T(128)} %bitcast.1.scale_ref, bf16[256,128]{1,0:T(8,128)(2,1)S(1)} %copy-done.9, bf16[256,128]{1,0:T(8,128)(2,1)S(1)} %copy-done.8, ...), custom_call_target="tpu_custom_call" | custom-call | flops 100000000 | bytes 2621444 | tf_op jit(solution)/shard_map/pallas_call | solution.py:407
  117.4 13.2 %all_to_all.94 = bf16[16,8,512]{2,1,0:T(8,128)(2,1)S(1)} all-to-all(bf16[16,8,512]{2,1,0:T(8,128)(2,1)S(1)} %bitcast.50), channel_id=1, replica_groups=mesh['gx'=16,'gy'=32] {'gx'}, dimensions={0} | all-to-all | bytes 262144 | tf_op jit(solution)/shard_map/all_to_all | solution.py:424
  130.6 0.2 shard_map.128
  130.8 0.0 copy-start.2
  130.9 18.7 %all_to_all.95 = bf16[32,8,512]{2,1,0:T(8,128)(2,1)S(1)} all-to-all(bf16[32,8,512]{2,1,0:T(8,128)(2,1)S(1)} %bitcast.37), channel_id=1, replica_groups={{0,1,2,3,16,17,18,19,8,9,10,11,24,25,26,27,4,5,6,7,20,21,22,23,12,13,14..., dimensions={0} | all-to-all | bytes 524288 | tf_op jit(solution)/shard_map/all_to_all | solution.py:424
  149.6 0.0 copy-done.2
  149.6 1.5 %shard_map.129 = bf16[2048,128]{1,0:T(8,128)(2,1)} custom-call(bf16[256,512]{1,0:T(8,128)(2,1)S(1)} %bitcast.40, bf16[4,128,512]{2,1,0:T(8,128)(2,1)S(1)} %get-tuple-element.21.slope_ref, bf16[16,16]{1,0:T(8,128)(2,1)S(1)} %copy-done.10, bf16[256,512]{1,0:T(8,128)(2,1)S(1)} %copy-done.2), custom_call_target="tpu_custom_call" | custom-call | flops 100000000 | bytes 1573376 | tf_op jit(solution)/shard_map/pallas_call | solution.py:407
Async XLA Ops:
  0.6 1.0 copy-start.1
  1.6 1.0 copy-start.3
  2.6 47.1 %copy-start = (bf16[16,16,4,1,512]{4,2,3,1,0:T(4,128)(2,1)S(1)}, bf16[16,16,4,1,512]{4,2,3,1,0:T(4,128)(2,1)}, u32[]{:S(2)}) copy-start(bf16[16,16,4,1,512]{4,2,3,1,0:T(4,128)(2,1)} %param.11) | copy-start | bytes 3145732
  3.9 24.7 %copy-start.7 = (bf16[128,256]{1,0:T(8,128)(2,1)S(1)}, bf16[128,256]{1,0:T(8,128)(2,1)}, u32[]{:S(2)}) copy-start(bf16[128,256]{1,0:T(8,128)(2,1)} %constant.24.clone.table_ref) | copy-start | bytes 196612
  29.0 20.7 %copy-start.8 = (bf16[256,128]{1,0:T(8,128)(2,1)S(1)}, bf16[256,128]{1,0:T(8,128)(2,1)}, u32[]{:S(2)}) copy-start(bf16[256,128]{1,0:T(8,128)(2,1)} %constant.27.clone.x_bwd_ref) | copy-start | bytes 196612
  29.1 20.7 %copy-start.9 = (bf16[256,128]{1,0:T(8,128)(2,1)S(1)}, bf16[256,128]{1,0:T(8,128)(2,1)}, u32[]{:S(2)}) copy-start(bf16[256,128]{1,0:T(8,128)(2,1)} %constant.26.clone.x_fwd_ref) | copy-start | bytes 196612
  49.8 14.8 %copy-start.6 = (bf16[256,128]{1,0:T(8,128)(2,1)S(1)}, bf16[256,128]{1,0:T(8,128)(2,1)}, u32[]{:S(2)}) copy-start(bf16[256,128]{1,0:T(8,128)(2,1)} %constant.25.clone.table_ref) | copy-start | bytes 196612
  51.2 32.3 %copy-start.5 = (bf16[1,4,16,8,4,128]{5,4,3,2,1,0:T(4,128)(2,1)S(1)}, bf16[1,4,16,8,4,128]{5,4,3,2,1,0:T(4,128)(2,1)}, u32[]{:S(2)}) copy-start(bf16[1,4,16,8,4,128]{5,4,3,2,1,0:T(4,128)(2,1)} %param.13) | copy-start | bytes 1572868
  64.5 18.9 %copy-start.4 = (bf16[1,4,16,8,4,128]{5,4,3,2,1,0:T(4,128)(2,1)S(1)}, bf16[1,4,16,8,4,128]{5,4,3,2,1,0:T(4,128)(2,1)}, u32[]{:S(2)}) copy-start(bf16[1,4,16,8,4,128]{5,4,3,2,1,0:T(4,128)(2,1)} %param.10) | copy-start | bytes 1572868
  64.8 18.7 %copy-start.10 = (bf16[16,16]{1,0:T(8,128)(2,1)S(1)}, bf16[16,16]{1,0:T(8,128)(2,1)}, u32[]{:S(2)}) copy-start(bf16[16,16]{1,0:T(8,128)(2,1)} %point_ref.3) | copy-start | bytes 1540
  130.8 18.7 %copy-start.2 = (bf16[256,512]{1,0:T(8,128)(2,1)S(1)}, bf16[256,512]{1,0:T(8,128)(2,1)}, u32[]{:S(2)}) copy-start(bf16[256,512]{1,0:T(8,128)(2,1)} %constant.23.clone.zt_hbm.zt_bwd_ref.zt_fwd_ref) | copy-start | bytes 786436

commit v2 on v1

--- a/solution.py
+++ b/solution.py
@@ -22,7 +22,7 @@
 YL = Y // GY
 JL = MY // GX
 LANES = 128
-GY_ORDER = [y * 4 + z for y in (0, 4, 2, 6, 1, 5, 3, 7) for z in range(4)]
+GX_ORDER = list(range(GX))[::-1]
 
 F32 = jnp.float32
 BF16 = jnp.bfloat16
@@ -47,7 +47,6 @@
     quarter = np.mod(np.arange(T)[:, None] * np.arange(T)[None, :], T)
     ct = np.array([1.0, 0.0, -1.0, 0.0])[quarter]
     st = np.array([0.0, 1.0, 0.0, -1.0])[quarter]
-    cz, sz = cz[GY_ORDER], sz[GY_ORDER]
     both_cos = (
         cz[None, :, None, :] * ct[:, None, :, None] - sz[None, :, None, :] * st[:, None, :, None]
     )
@@ -63,14 +62,14 @@
     fwd[:, 0, :, 1] = sy
     fwd[:, 1, :, 0] = -sy
     fwd[:, 1, :, 1] = cy
-    fwd = fwd.reshape(MY * 2, GY, YL * 2)[:, GY_ORDER]
-    y_fwd = fwd.reshape(GX, JL, 2, Y * 2).transpose(1, 2, 0, 3).reshape(MY * 2, Y * 2)
+    fwd = fwd.reshape(GX, JL, 2, Y * 2)[GX_ORDER]
+    y_fwd = fwd.transpose(1, 2, 0, 3).reshape(MY * 2, Y * 2)
     bwd = np.empty((Y, 2, MY, 2))
     bwd[:, 0, :, 0] = cy.T
     bwd[:, 0, :, 1] = -sy.T
     bwd[:, 1, :, 0] = sy.T
     bwd[:, 1, :, 1] = cy.T
-    y_bwd = bwd.reshape(GY, YL * 2, MY * 2)[GY_ORDER].reshape(Y * 2, MY * 2)
+    y_bwd = bwd.reshape(Y * 2, GX, JL * 2)[:, GX_ORDER].reshape(Y * 2, MY * 2)
 
     cx, sx = (a.astype(np.float64) for a in cos_sin(signed(MX), X))
     fwd = np.empty((X, 2, 2, MX))
@@ -78,13 +77,14 @@
     fwd[:, 1, 0, :] = sx.T
     fwd[:, 0, 1, :] = -sx.T
     fwd[:, 1, 1, :] = cx.T
-    x_fwd = fwd.reshape(X * 2, 2 * MX)
+    x_fwd = fwd.reshape(GX, XL * 2, 2 * MX)[GX_ORDER].reshape(X * 2, 2 * MX)
     bwd = np.empty((X, 2, 2, MX))
     bwd[:, 0, 0, :] = cx.T
     bwd[:, 0, 1, :] = -sx.T
     bwd[:, 1, 0, :] = sx.T
     bwd[:, 1, 1, :] = cx.T
-    x_bwd = bwd.reshape(GX, XL, 2, 2 * MX).transpose(1, 2, 0, 3).reshape(X * 2, 2 * MX)
+    bwd = bwd.reshape(GX, XL, 2, 2 * MX)[GX_ORDER]
+    x_bwd = bwd.transpose(1, 2, 0, 3).reshape(X * 2, 2 * MX)
     return tuple(a.astype(BF16) for a in (zt_fwd, zt_bwd, y_fwd, y_bwd, x_fwd, x_bwd))
 
 
@@ -112,13 +112,11 @@
 
 
 def gelu_parts(pre):
-    inner = root_two_over_pi * (pre + gelu_cubic * pre * pre * pre)
-    hyper = jnp.tanh(inner)
-    value = 0.5 * pre * (1.0 + hyper)
-    slope = 0.5 * (1.0 + hyper) + 0.5 * pre * (1.0 - hyper * hyper) * root_two_over_pi * (
-        1.0 + 3.0 * gelu_cubic * pre * pre
-    )
-    return value, slope
+    square = pre * pre
+    inner = pre * (root_two_over_pi + (root_two_over_pi * gelu_cubic) * square)
+    half = 0.5 + 0.5 * jnp.tanh(inner)
+    rise = pre * (2.0 * root_two_over_pi + (6.0 * root_two_over_pi * gelu_cubic) * square)
+    return pre * half, half * (1.0 + (1.0 - half) * rise)
 
 
 def cells_of(wide_ref, y):
@@ -161,20 +159,10 @@
     )
 
 
-def open_kernel(field_hbm, zt_hbm, out_ref, field, zt_fwd, wide, spread, sems):
-    rows = C * XL * YL
-    copies = [pltpu.make_async_copy(zt_hbm, zt_fwd, sems.at[T])]
-    for t in range(T):
-        part = pl.ds(t * rows, rows)
-        copies.append(pltpu.make_async_copy(field_hbm.at[part], field.at[part], sems.at[t]))
-    for copy in copies:
-        copy.start()
-    for t in range(T):
-        copies[1 + t].wait()
-        wide[t * rows : (t + 1) * rows] = field[t * rows : (t + 1) * rows].astype(F32)
-    copies[0].wait()
+def open_kernel(field_ref, zt_fwd_ref, out_ref, wide, spread):
+    wide[...] = field_ref[...].astype(F32)
     for y in range(YL):
-        put_modes(spread, y, cells_of(wide, y).astype(BF16), zt_fwd[...])
+        put_modes(spread, y, cells_of(wide, y).astype(BF16), zt_fwd_ref[...])
     pack(spread, out_ref)
 
 
@@ -324,41 +312,32 @@
 
 def cell_kernel(
     in_ref,
-    field_hbm,
-    cotangent_hbm,
+    field_ref,
+    cotangent_ref,
     point_ref,
     zt_bwd_ref,
     zt_fwd_ref,
     out_ref,
     slope_ref,
     layer_hbm,
-    field,
-    cotangent,
     wide,
     other,
     spread,
-    sems,
+    layer,
+    sem,
 ):
-    copies = [
-        pltpu.make_async_copy(field_hbm, field, sems.at[0]),
-        pltpu.make_async_copy(cotangent_hbm, cotangent, sems.at[1]),
-    ]
-    for copy in copies:
-        copy.start()
     point = point_table(point_ref, False)
     unpack(in_ref, spread)
     modes = [modes_of(spread, y).astype(BF16) for y in range(YL)]
-    copies[0].wait()
-    wide[...] = field[...].astype(F32)
-    copies[1].wait()
-    other[...] = cotangent[...].astype(F32)
+    wide[...] = field_ref[...].astype(F32)
+    other[...] = cotangent_ref[...].astype(F32)
     for y in range(YL):
         pre = dot(modes[y], zt_bwd_ref[...], 0, 0) + dot(point, cells_of(wide, y).astype(BF16))
         value, slope = gelu_parts(pre)
         put_cells(wide, y, value)
         slope_ref[y] = (cells_of(other, y) * slope).astype(BF16)
-    field[...] = wide[...].astype(BF16)
-    send = pltpu.make_async_copy(field, layer_hbm, sems.at[2])
+    layer[...] = wide[...].astype(BF16)
+    send = pltpu.make_async_copy(layer, layer_hbm, sem)
     send.start()
     for y in range(YL):
         put_modes(spread, y, slope_ref[y], zt_fwd_ref[...])
@@ -366,13 +345,20 @@
     send.wait()
 
 
-def close_kernel(in_ref, slope_ref, point_ref, zt_bwd_ref, out_ref, spread, wide):
+def close_kernel(in_ref, slope_ref, point_ref, zt_bwd_ref, out_hbm, spread, wide, out, sems):
     point = point_table(point_ref, True)
     unpack(in_ref, spread)
     for y in range(YL):
         modes = modes_of(spread, y).astype(BF16)
         put_cells(wide, y, dot(modes, zt_bwd_ref[...], 0, 0) + dot(point, slope_ref[y]))
-    out_ref[...] = wide[...].astype(BF16)
+    copies = []
+    for t in range(T):
+        rows = pl.ds(t * C * XL * YL, C * XL * YL)
+        out[rows, :] = wide[rows, :].astype(BF16)
+        copies.append(pltpu.make_async_copy(out.at[rows], out_hbm.at[rows], sems.at[t]))
+        copies[t].start()
+    for copy in copies:
+        copy.wait()
 
 
 ROWS = T * C * XL * YL
@@ -394,13 +380,11 @@
     return pltpu.VMEM(shape, dtype)
 
 
-def call(kernel, outs, operands, scratch=(), scalars=(), far=(), far_outs=(), flops=10**8):
+def call(kernel, outs, operands, scratch=(), scalars=(), far_outs=(), flops=10**8):
     near = pl.BlockSpec(memory_space=pltpu.VMEM)
     smem = pl.BlockSpec(memory_space=pltpu.SMEM)
     anywhere = pl.BlockSpec(memory_space=pltpu.HBM)
-    specs = [
-        smem if i in scalars else anywhere if i in far else near for i in range(len(operands))
-    ]
+    specs = [smem if i in scalars else near for i in range(len(operands))]
     out_specs = tuple(anywhere if i in far_outs else near for i in range(len(outs)))
     single = len(outs) == 1
     moved = sum(math.prod(o.shape) * o.dtype.itemsize for o in list(outs) + list(operands))
@@ -420,16 +404,15 @@
 
 
 def exchange(block, axis):
-    groups = [GY_ORDER] if axis == "gy" else None
+    groups = [GX_ORDER] if axis == "gx" else None
     return lax.all_to_all(
         block, axis, split_axis=0, concat_axis=0, axis_index_groups=groups, tiled=True
     )
 
 
 def open_stage(field, zt_fwd):
-    scratch = [vmem(WIDE, BF16), vmem(ZT, BF16), vmem(WIDE), vmem(ZT_SPREAD)]
-    scratch.append(pltpu.SemaphoreType.DMA((T + 1,)))
-    return call(open_kernel, [shaped(ZT)], [field, zt_fwd], scratch, far=(0, 1))
+    scratch = [vmem(WIDE), vmem(ZT_SPREAD)]
+    return call(open_kernel, [shaped(ZT)], [field, zt_fwd], scratch)
 
 
 def y_forward_stage(block, y_fwd):
@@ -451,14 +434,13 @@
 
 
 def cell_stage(block, field, cotangent, point_weight, zt_bwd, zt_fwd):
-    scratch = [vmem(WIDE, BF16), vmem(WIDE, BF16), vmem(WIDE), vmem(WIDE), vmem(ZT_SPREAD)]
-    scratch.append(pltpu.SemaphoreType.DMA((3,)))
+    scratch = [vmem(WIDE), vmem(WIDE), vmem(ZT_SPREAD), vmem(WIDE, BF16)]
+    scratch.append(pltpu.SemaphoreType.DMA)
     return call(
         cell_kernel,
         [shaped(ZT), shaped(CELLS), shaped(WIDE)],
         [block, field, cotangent, point_weight, zt_bwd, zt_fwd],
         scratch,
-        far=(1, 2),
         far_outs=(2,),
     )
 
@@ -480,7 +462,8 @@
         close_kernel,
         [shaped(WIDE)],
         [block, slope, point_weight, zt_bwd],
-        [vmem(ZT_SPREAD), vmem(WIDE)],
+        [vmem(ZT_SPREAD), vmem(WIDE), vmem(WIDE, BF16), pltpu.SemaphoreType.DMA((T,))],
+        far_outs=(0,),
     )
 
 

time: 152 us -> 143 us (0.941)
  blocking collectives: 139 us -> 131 us
    all_to_all x8, blocking collectives: 139 us -> 131 us  [exchange(): lax.all_to_all(block, axis, split_axis=0, concat_axis=0, axis_index_group...]
where the time goes in v2:
time: 143 us
  blocking collectives  131 us (92%)
  Pallas kernels  8.56 us (6%)
  local copies, waits for them, and re-layouts  2.04 us (1%)
    all_to_all x8, blocking collectives, exchange(): lax.all_to_all(block, axis, split_axis=0, concat_axis=0, axis_index_group...  131 us
    pallas_call x9, Pallas kernels, call(): pl.pallas_call(kernel, out_shape=outs[0] if single else tuple(outs), in_s...  8.56 us

profile of v2, /device:TPU:8, one launch (start us, length us, event | category | flops | bytes accessed | tf_op | source)
XLA Modules:
  0.0 142.7 jit_solution(4738704385195732827)
XLA Ops:
  0.6 0.0 copy-start.1
  0.7 0.9 copy-done.1
  1.6 0.0 copy-start.3
  1.6 1.0 copy-done.3
  2.6 0.0 copy-start
  2.6 0.5 shard_map.121
  3.1 0.0 copy-start.7
  3.1 25.8 %all_to_all.88 = bf16[32,8,512]{2,1,0:T(8,128)(2,1)S(1)} all-to-all(bf16[32,8,512]{2,1,0:T(8,128)(2,1)S(1)} %bitcast.41), channel_id=1, replica_groups=mesh['gx'=16,'gy'=32] {'gy'}, dimensions={0} | all-to-all | bytes 524288 | tf_op jit(solution)/shard_map/all_to_all | solution.py:408
  28.9 0.0 copy-done.7
  28.9 0.5 shard_map.122
  29.4 0.0 copy-start.8
  29.4 0.0 copy-start.9
  29.4 14.5 %all_to_all.89 = bf16[16,16,256]{2,1,0:T(8,128)(2,1)S(1)} all-to-all(bf16[16,16,256]{2,1,0:T(8,128)(2,1)S(1)} %bitcast.46), channel_id=1, replica_groups={{480,448,416,384,352,320,288,256,224,192,160,128,96,64,32,0},{481,449,4..., dimensions={0} | all-to-all | bytes 262144 | tf_op jit(solution)/shard_map/all_to_all | solution.py:408
  43.9 0.0 copy-done
  43.9 0.0 copy-done.8
  43.9 0.0 copy-done.9
  43.9 0.0 copy-start.6
  43.9 1.4 shard_map.123
  45.4 0.0 copy-start.5
  45.4 12.7 %all_to_all.90 = bf16[16,8,512]{2,1,0:T(8,128)(2,1)S(1)} all-to-all(bf16[16,8,512]{2,1,0:T(8,128)(2,1)S(1)} %bitcast.51), channel_id=1, replica_groups={{480,448,416,384,352,320,288,256,224,192,160,128,96,64,32,0},{481,449,4..., dimensions={0} | all-to-all | bytes 262144 | tf_op jit(solution)/shard_map/all_to_all | solution.py:408
  58.0 0.0 copy-start.4
  58.0 0.0 copy-done.6
  58.0 0.2 shard_map.124
  58.3 0.0 copy-start.10
  58.3 18.4 %all_to_all.91 = bf16[32,8,512]{2,1,0:T(8,128)(2,1)S(1)} all-to-all(bf16[32,8,512]{2,1,0:T(8,128)(2,1)S(1)} %bitcast.39), channel_id=1, replica_groups=mesh['gx'=16,'gy'=32] {'gy'}, dimensions={0} | all-to-all | bytes 524288 | tf_op jit(solution)/shard_map/all_to_all | solution.py:408
  76.6 0.0 copy-done.5
  76.6 0.0 copy-done.4
  76.6 0.0 copy-done.10
  76.7 2.1 %shard_map.125 = (bf16[256,512]{1,0:T(8,128)(2,1)S(1)}, bf16[4,128,512]{2,1,0:T(8,128)(2,1)S(1)}, bf16[2048,128]{1,0:T(8,128)(2,1)}) custom-call(bf16[256,512]{1,0:T(8,128)(2,1)S(1)} %bitcast.35, bf16[2048,128]{1,0:T(8,128)(2,1)S(1)} %bitcast.34, bf16[2048,128]{1,0:T(8,128)(2,1)S(1)} %bitcast.42, bf16[16,16]{1,0:T(8,128)(2,1)S(1)} %copy-done.10, ...), custom_call_target="tpu_custom_call" | custom-call | flops 100000000 | bytes 3146240 | tf_op jit(solution)/shard_map/pallas_call | solution.py:391
  78.7 16.4 %all_to_all.92 = bf16[32,8,512]{2,1,0:T(8,128)(2,1)S(1)} all-to-all(bf16[32,8,512]{2,1,0:T(8,128)(2,1)S(1)} %bitcast.49), channel_id=1, replica_groups=mesh['gx'=16,'gy'=32] {'gy'}, dimensions={0} | all-to-all | bytes 524288 | tf_op jit(solution)/shard_map/all_to_all | solution.py:408
  95.1 0.5 shard_map.126
  95.6 12.5 %all_to_all.93 = bf16[16,16,256]{2,1,0:T(8,128)(2,1)S(1)} all-to-all(bf16[16,16,256]{2,1,0:T(8,128)(2,1)S(1)} %bitcast.44), channel_id=1, replica_groups={{480,448,416,384,352,320,288,256,224,192,160,128,96,64,32,0},{481,449,4..., dimensions={0} | all-to-all | bytes 262144 | tf_op jit(solution)/shard_map/all_to_all | solution.py:408
  108.1 1.7 %shard_map.127 = (bf16[128,512]{1,0:T(8,128)(2,1)S(1)}, bf16[16,256,128]{2,1,0:T(8,128)(2,1)}) custom-call(bf16[256,256]{1,0:T(8,128)(2,1)S(1)} %bitcast.48, bf16[16,256,128]{2,1,0:T(8,128)(2,1)S(1)} %bitcast.32, f32[1]{0:T(128)} %bitcast.1.scale_ref, bf16[256,128]{1,0:T(8,128)(2,1)S(1)} %copy-done.9, bf16[256,128]{1,0:T(8,128)(2,1)S(1)} %copy-done.8, ...), custom_call_target="tpu_custom_call" | custom-call | flops 100000000 | bytes 2621444 | tf_op jit(solution)/shard_map/pallas_call | solution.py:391
  109.8 12.5 %all_to_all.94 = bf16[16,8,512]{2,1,0:T(8,128)(2,1)S(1)} all-to-all(bf16[16,8,512]{2,1,0:T(8,128)(2,1)S(1)} %bitcast.50), channel_id=1, replica_groups={{480,448,416,384,352,320,288,256,224,192,160,128,96,64,32,0},{481,449,4..., dimensions={0} | all-to-all | bytes 262144 | tf_op jit(solution)/shard_map/all_to_all | solution.py:408
  122.4 0.2 shard_map.128
  122.6 0.0 copy-start.2
  122.6 18.6 %all_to_all.95 = bf16[32,8,512]{2,1,0:T(8,128)(2,1)S(1)} all-to-all(bf16[32,8,512]{2,1,0:T(8,128)(2,1)S(1)} %bitcast.37), channel_id=1, replica_groups=mesh['gx'=16,'gy'=32] {'gy'}, dimensions={0} | all-to-all | bytes 524288 | tf_op jit(solution)/shard_map/all_to_all | solution.py:408
  141.2 0.0 copy-done.2
  141.2 1.5 %shard_map.129 = bf16[2048,128]{1,0:T(8,128)(2,1)} custom-call(bf16[256,512]{1,0:T(8,128)(2,1)S(1)} %bitcast.40, bf16[4,128,512]{2,1,0:T(8,128)(2,1)S(1)} %get-tuple-element.21.slope_ref, bf16[16,16]{1,0:T(8,128)(2,1)S(1)} %copy-done.10, bf16[256,512]{1,0:T(8,128)(2,1)S(1)} %copy-done.2), custom_call_target="tpu_custom_call" | custom-call | flops 100000000 | bytes 1573376 | tf_op jit(solution)/shard_map/pallas_call | solution.py:391
Async XLA Ops:
  0.6 1.0 copy-start.1
  1.6 1.0 copy-start.3
  2.6 41.3 %copy-start = (bf16[16,16,4,1,512]{4,2,3,1,0:T(4,128)(2,1)S(1)}, bf16[16,16,4,1,512]{4,2,3,1,0:T(4,128)(2,1)}, u32[]{:S(2)}) copy-start(bf16[16,16,4,1,512]{4,2,3,1,0:T(4,128)(2,1)} %param.11) | copy-start | bytes 3145732
  3.1 25.8 %copy-start.7 = (bf16[128,256]{1,0:T(8,128)(2,1)S(1)}, bf16[128,256]{1,0:T(8,128)(2,1)}, u32[]{:S(2)}) copy-start(bf16[128,256]{1,0:T(8,128)(2,1)} %constant.24.clone.table_ref) | copy-start | bytes 196612
  29.4 14.6 %copy-start.8 = (bf16[256,128]{1,0:T(8,128)(2,1)S(1)}, bf16[256,128]{1,0:T(8,128)(2,1)}, u32[]{:S(2)}) copy-start(bf16[256,128]{1,0:T(8,128)(2,1)} %constant.27.clone.x_bwd_ref) | copy-start | bytes 196612
  29.4 14.5 %copy-start.9 = (bf16[256,128]{1,0:T(8,128)(2,1)S(1)}, bf16[256,128]{1,0:T(8,128)(2,1)}, u32[]{:S(2)}) copy-start(bf16[256,128]{1,0:T(8,128)(2,1)} %constant.26.clone.x_fwd_ref) | copy-start | bytes 196612
  43.9 14.1 %copy-start.6 = (bf16[256,128]{1,0:T(8,128)(2,1)S(1)}, bf16[256,128]{1,0:T(8,128)(2,1)}, u32[]{:S(2)}) copy-start(bf16[256,128]{1,0:T(8,128)(2,1)} %constant.25.clone.table_ref) | copy-start | bytes 196612
  45.4 31.3 %copy-start.5 = (bf16[1,4,16,8,4,128]{5,4,3,2,1,0:T(4,128)(2,1)S(1)}, bf16[1,4,16,8,4,128]{5,4,3,2,1,0:T(4,128)(2,1)}, u32[]{:S(2)}) copy-start(bf16[1,4,16,8,4,128]{5,4,3,2,1,0:T(4,128)(2,1)} %param.13) | copy-start | bytes 1572868
  58.0 18.6 %copy-start.4 = (bf16[1,4,16,8,4,128]{5,4,3,2,1,0:T(4,128)(2,1)S(1)}, bf16[1,4,16,8,4,128]{5,4,3,2,1,0:T(4,128)(2,1)}, u32[]{:S(2)}) copy-start(bf16[1,4,16,8,4,128]{5,4,3,2,1,0:T(4,128)(2,1)} %param.10) | copy-start | bytes 1572868
  58.3 18.4 %copy-start.10 = (bf16[16,16]{1,0:T(8,128)(2,1)S(1)}, bf16[16,16]{1,0:T(8,128)(2,1)}, u32[]{:S(2)}) copy-start(bf16[16,16]{1,0:T(8,128)(2,1)} %point_ref.3) | copy-start | bytes 1540
  122.6 18.6 %copy-start.2 = (bf16[256,512]{1,0:T(8,128)(2,1)S(1)}, bf16[256,512]{1,0:T(8,128)(2,1)}, u32[]{:S(2)}) copy-start(bf16[256,512]{1,0:T(8,128)(2,1)} %constant.23.clone.zt_fwd_ref.zt_bwd_ref) | copy-start | bytes 786436

commit v3 on v2

--- a/solution.py
+++ b/solution.py
@@ -159,11 +159,35 @@
     )
 
 
-def open_kernel(field_ref, zt_fwd_ref, out_ref, wide, spread):
+def build_zt(table):
+    shape = (MZ, Z)
+    turns = lax.broadcasted_iota(jnp.int32, shape, 0) * lax.broadcasted_iota(jnp.int32, shape, 1)
+    angle = (turns & (Z - 1)).astype(F32) * (2.0 * math.pi / Z)
+    cosine = jnp.cos(angle)
+    sine = jnp.sin(angle)
+    real = (cosine, -sine, -cosine, sine)
+    imag = (-sine, -cosine, sine, cosine)
+    for kt in range(T):
+        for p, part in enumerate((real, imag)):
+            row = (kt * 2 + p) * MZ
+            for t in range(T):
+                table[row : row + MZ, t * Z : (t + 1) * Z] = part[kt * t % T].astype(BF16)
+
+
+def open_kernel(field_ref, out_ref, wide, spread, table):
+    build_zt(table)
     wide[...] = field_ref[...].astype(F32)
     for y in range(YL):
-        put_modes(spread, y, cells_of(wide, y).astype(BF16), zt_fwd_ref[...])
+        put_modes(spread, y, cells_of(wide, y).astype(BF16), table[...])
     pack(spread, out_ref)
+
+
+def split_kernel(field_ref, cotangent_ref, field_out, cotangent_out, wide, other):
+    wide[...] = field_ref[...].astype(F32)
+    other[...] = cotangent_ref[...].astype(F32)
+    for y in range(YL):
+        field_out[y] = cells_of(wide, y).astype(BF16)
+        cotangent_out[y] = cells_of(other, y).astype(BF16)
 
 
 def y_forward_kernel(in_ref, table_ref, out_ref, spread):
@@ -216,11 +240,23 @@
 
 
 def mix_kernel(
-    in_ref, w_ref, scale_ref, x_fwd_ref, x_bwd_ref, out_ref, real_ref, imag_ref, spread
+    in_ref,
+    w_ref,
+    scale_ref,
+    x_fwd_ref,
+    x_bwd_ref,
+    out_ref,
+    real_out,
+    imag_out,
+    real_ref,
+    imag_ref,
+    spread,
 ):
     real, imag = to_spectrum(in_ref, x_fwd_ref)
     real_ref[...] = real
     imag_ref[...] = imag
+    real_out[...] = real.astype(BF16)
+    imag_out[...] = imag.astype(BF16)
 
     def add(c, total):
         s_real = at_channel(real_ref, c)[None]
@@ -249,36 +285,20 @@
     scale_ref,
     x_fwd_ref,
     x_bwd_ref,
-    s_real_ref,
-    s_imag_ref,
     out_ref,
-    grad_hbm,
+    real_out,
+    imag_out,
     real_ref,
     imag_ref,
     back_real,
     back_imag,
     spread,
-    grad,
-    sem,
 ):
     real, imag = to_spectrum(in_ref, x_fwd_ref)
     real_ref[...] = real
     imag_ref[...] = imag
-
-    def outer(c, carry):
-        s_real = (at_channel(s_real_ref, c).astype(F32) * scale_ref[0])[None, None]
-        s_imag = (at_channel(s_imag_ref, c).astype(F32) * scale_ref[0])[None, None]
-        a_real = real_ref[...].reshape(C, 1, 8, LANES)
-        a_imag = imag_ref[...].reshape(C, 1, 8, LANES)
-        both = jnp.concatenate(
-            [s_real * a_real + s_imag * a_imag, s_real * a_imag - s_imag * a_real], 1
-        )
-        grad[c] = both.reshape(C * 2 * 8, LANES).astype(BF16)
-        return carry
-
-    lax.fori_loop(0, C, outer, 0)
-    send = pltpu.make_async_copy(grad, grad_hbm, sem)
-    send.start()
+    real_out[...] = real.astype(BF16)
+    imag_out[...] = imag.astype(BF16)
 
     def one(c, carry):
         a_real = real_ref[...].reshape(C, 8, LANES)
@@ -292,7 +312,29 @@
     lax.fori_loop(0, C, one, 0)
     scale = scale_ref[0]
     from_spectrum(back_real[...] * scale, back_imag[...] * scale, x_bwd_ref, out_ref, spread)
-    send.wait()
+
+
+def grad_kernel(
+    s_real_in, s_imag_in, a_real_in, a_imag_in, scale_ref, out_ref, s_real, s_imag, a_real, a_imag
+):
+    scale = scale_ref[0]
+    s_real[...] = s_real_in[...].astype(F32) * scale
+    s_imag[...] = s_imag_in[...].astype(F32) * scale
+    a_real[...] = a_real_in[...].astype(F32)
+    a_imag[...] = a_imag_in[...].astype(F32)
+
+    def one(c, carry):
+        c_real = at_channel(s_real, c)[None, None]
+        c_imag = at_channel(s_imag, c)[None, None]
+        o_real = a_real[...].reshape(C, 1, 8, LANES)
+        o_imag = a_imag[...].reshape(C, 1, 8, LANES)
+        both = jnp.concatenate(
+            [c_real * o_real + c_imag * o_imag, c_real * o_imag - c_imag * o_real], 1
+        )
+        out_ref[c] = both.reshape(C * 2 * 8, LANES).astype(BF16)
+        return carry
+
+    lax.fori_loop(0, C, one, 0)
 
 
 def y_backward_kernel(in_ref, table_ref, out_ref):
@@ -319,30 +361,26 @@
     zt_fwd_ref,
     out_ref,
     slope_ref,
-    layer_hbm,
-    wide,
-    other,
+    layer_ref,
     spread,
-    layer,
-    sem,
 ):
     point = point_table(point_ref, False)
     unpack(in_ref, spread)
     modes = [modes_of(spread, y).astype(BF16) for y in range(YL)]
-    wide[...] = field_ref[...].astype(F32)
-    other[...] = cotangent_ref[...].astype(F32)
     for y in range(YL):
-        pre = dot(modes[y], zt_bwd_ref[...], 0, 0) + dot(point, cells_of(wide, y).astype(BF16))
+        pre = dot(modes[y], zt_bwd_ref[...], 0, 0) + dot(point, field_ref[y])
         value, slope = gelu_parts(pre)
-        put_cells(wide, y, value)
-        slope_ref[y] = (cells_of(other, y) * slope).astype(BF16)
-    layer[...] = wide[...].astype(BF16)
-    send = pltpu.make_async_copy(layer, layer_hbm, sem)
-    send.start()
+        layer_ref[y] = value.astype(BF16)
+        slope_ref[y] = (cotangent_ref[y].astype(F32) * slope).astype(BF16)
     for y in range(YL):
         put_modes(spread, y, slope_ref[y], zt_fwd_ref[...])
     pack(spread, out_ref)
-    send.wait()
+
+
+def layer_kernel(layer_ref, out_ref, wide):
+    for y in range(YL):
+        put_cells(wide, y, layer_ref[y].astype(F32))
+    out_ref[...] = wide[...].astype(BF16)
 
 
 def close_kernel(in_ref, slope_ref, point_ref, zt_bwd_ref, out_hbm, spread, wide, out, sems):
@@ -410,9 +448,15 @@
     )
 
 
-def open_stage(field, zt_fwd):
-    scratch = [vmem(WIDE), vmem(ZT_SPREAD)]
-    return call(open_kernel, [shaped(ZT)], [field, zt_fwd], scratch)
+def open_stage(field):
+    scratch = [vmem(WIDE), vmem(ZT_SPREAD), vmem((T * 2 * MZ, T * Z), BF16)]
+    return call(open_kernel, [shaped(ZT)], [field], scratch)
+
+
+def split_stage(field, cotangent):
+    return call(
+        split_kernel, [shaped(CELLS)] * 2, [field, cotangent], [vmem(WIDE), vmem(WIDE)]
+    )
 
 
 def y_forward_stage(block, y_fwd):
@@ -422,9 +466,9 @@
 def mix_stage(block, weight, scale, x_fwd, x_bwd):
     return call(
         mix_kernel,
-        [shaped(AFTER_X), shaped(PARTS, F32), shaped(PARTS, F32)],
+        [shaped(AFTER_X), shaped(PARTS), shaped(PARTS)],
         [block, weight, scale, x_fwd, x_bwd],
-        [vmem(X_SPREAD)],
+        [vmem(PARTS), vmem(PARTS), vmem(X_SPREAD)],
         scalars=(2,),
     )
 
@@ -434,26 +478,31 @@
 
 
 def cell_stage(block, field, cotangent, point_weight, zt_bwd, zt_fwd):
-    scratch = [vmem(WIDE), vmem(WIDE), vmem(ZT_SPREAD), vmem(WIDE, BF16)]
-    scratch.append(pltpu.SemaphoreType.DMA)
     return call(
         cell_kernel,
-        [shaped(ZT), shaped(CELLS), shaped(WIDE)],
+        [shaped(ZT), shaped(CELLS), shaped(CELLS)],
         [block, field, cotangent, point_weight, zt_bwd, zt_fwd],
-        scratch,
-        far_outs=(2,),
-    )
-
-
-def back_stage(block, weight, scale, x_fwd, x_bwd, spec_real, spec_imag):
-    scratch = [vmem(PARTS)] * 4 + [vmem(X_SPREAD), vmem(GRAD, BF16), pltpu.SemaphoreType.DMA]
+        [vmem(ZT_SPREAD)],
+    )
+
+
+def layer_stage(layer):
+    return call(layer_kernel, [shaped(WIDE)], [layer], [vmem(WIDE)])
+
+
+def back_stage(block, weight, scale, x_fwd, x_bwd):
     return call(
         back_kernel,
-        [shaped(AFTER_X), shaped(GRAD)],
-        [block, weight, scale, x_fwd, x_bwd, spec_real, spec_imag],
-        scratch,
+        [shaped(AFTER_X), shaped(PARTS), shaped(PARTS)],
+        [block, weight, scale, x_fwd, x_bwd],
+        [vmem(PARTS)] * 4 + [vmem(X_SPREAD)],
         scalars=(2,),
-        far_outs=(1,),
+    )
+
+
+def grad_stage(spec, adj, scale):
+    return call(
+        grad_kernel, [shaped(GRAD)], [*spec, *adj, scale], [vmem(PARTS)] * 4, scalars=(4,)
     )
 
 
@@ -475,19 +524,20 @@
     kz = lax.axis_index("gy")
     scale = (jnp.where(kz == 0, 1.0, 2.0).astype(F32) / float(X * Y * Z * T)).reshape(1)
 
-    opened = open_stage(field, zt_fwd)
+    opened = open_stage(field)
     opened, scale = lax.optimization_barrier((opened, scale))
     halved = y_forward_stage(exchange(opened, "gy"), y_fwd)
-    mixed, spec_real, spec_imag = mix_stage(exchange(halved, "gx"), weight, scale, x_fwd, x_bwd)
+    mixed, *spec = mix_stage(exchange(halved, "gx"), weight, scale, x_fwd, x_bwd)
     along_y = y_backward_stage(exchange(mixed, "gx"), y_bwd)
-    turned, slope, layer_out = cell_stage(
+    field, cotan = split_stage(field, cotan)
+    turned, slope, layer = cell_stage(
         exchange(along_y, "gy"), field, cotan, point_weight, zt_bwd, zt_fwd
     )
     halved = y_forward_stage(exchange(turned, "gy"), y_fwd)
-    back, grad_spectral = back_stage(
-        exchange(halved, "gx"), weight, scale, x_fwd, x_bwd, spec_real, spec_imag
-    )
+    back, *adj = back_stage(exchange(halved, "gx"), weight, scale, x_fwd, x_bwd)
     along_y = y_backward_stage(exchange(back, "gx"), y_bwd)
+    layer_out = layer_stage(layer)
+    grad_spectral = grad_stage(spec, adj, scale)
     grad_field = close_stage(exchange(along_y, "gy"), slope, point_weight, zt_bwd)
 
     grad_spectral = (

time: 143 us -> 144 us (level)
  blocking collectives: 131 us -> 94.4 us
  waiting for transfers between devices: 0 us -> 22.2 us
  starting transfers between devices: 0 us -> 11.3 us
  Pallas kernels: 8.56 us -> 11.6 us
    all_to_all x8 -> x6, blocking collectives: 131 us -> 94.4 us  [exchange(): lax.all_to_all(block, axis, split_axis=0, concat_axis=0, axis_index_group...]
    all_to_all x0 -> x2, waiting for transfers between devices: none -> 22.2 us  [exchange(): lax.all_to_all(block, axis, split_axis=0, concat_axis=0, axis_index_group...]
    all_to_all x0 -> x2, starting transfers between devices: none -> 11.3 us  [exchange(): lax.all_to_all(block, axis, split_axis=0, concat_axis=0, axis_index_group...]
    pallas_call x9 -> x12, Pallas kernels: 8.56 us -> 11.6 us  [call(): pl.pallas_call(kernel, out_shape=outs[0] if single else tuple(outs), in_s...]
    unnamed x22 -> x24, local copies, waits for them, and re-layouts: 2.04 us -> 3 us
  transfers between devices with their start and end apart: 0 -> 2, of which waited for: 0 -> 2; matrix products, arithmetic and copies ran while one was open for 0% -> 0% of each run, Pallas kernels for 0% -> 2%
where the time goes in v3:
time: 144 us; the launch traced here: 143 us
  blocking collectives  94.4 us (66%)
  waiting for transfers between devices  22.2 us (15%)
  Pallas kernels  11.6 us (8%)
  starting transfers between devices  11.3 us (8%)
  local copies, waits for them, and re-layouts  3 us (2%)
    all_to_all x6, blocking collectives, exchange(): lax.all_to_all(block, axis, split_axis=0, concat_axis=0, axis_index_group...  94.4 us
    all_to_all x2, waiting for transfers between devices, exchange(): lax.all_to_all(block, axis, split_axis=0, concat_axis=0, axis_index_group...  22.2 us
    pallas_call x12, Pallas kernels, call(): pl.pallas_call(kernel, out_shape=outs[0] if single else tuple(outs), in_s...  11.6 us
    all_to_all x2, starting transfers between devices, exchange(): lax.all_to_all(block, axis, split_axis=0, concat_axis=0, axis_index_group...  11.3 us
    unnamed x24, local copies, waits for them, and re-layouts  3 us
  transfers between devices with their start and end apart: 2, of which 2 were waited for; matrix products, arithmetic and copies ran while one was open for 0% of the time, Pallas kernels for 2%

profile of v3, /device:TPU:8, one launch (start us, length us, event | category | flops | bytes accessed | tf_op | source)
XLA Modules:
  0.0 143.3 jit_solution(13273727327447560065)
XLA Ops:
  0.6 0.0 copy-start
  0.6 0.0 copy-start.2
  0.7 1.1 copy-done.2
  1.8 0.6 shard_map.121
  2.4 0.0 copy-start.10
  2.4 25.8 %all_to_all.88 = bf16[32,8,512]{2,1,0:T(8,128)(2,1)S(1)} all-to-all(bf16[32,8,512]{2,1,0:T(8,128)(2,1)S(1)} %bitcast.36), channel_id=1, replica_groups=mesh['gx'=16,'gy'=32] {'gy'}, dimensions={0} | all-to-all | bytes 524288 | tf_op jit(solution)/shard_map/all_to_all | solution.py:446
  28.1 0.0 copy-done.10
  28.1 0.5 shard_map.122
  28.6 0.0 copy-start.8
  28.6 0.0 copy-start.9
  28.6 14.5 %all_to_all.89 = bf16[16,16,256]{2,1,0:T(8,128)(2,1)S(1)} all-to-all(bf16[16,16,256]{2,1,0:T(8,128)(2,1)S(1)} %bitcast.44), channel_id=1, replica_groups={{480,448,416,384,352,320,288,256,224,192,160,128,96,64,32,0},{481,449,4..., dimensions={0} | all-to-all | bytes 262144 | tf_op jit(solution)/shard_map/all_to_all | solution.py:446
  43.1 0.0 copy-done
  43.1 0.0 copy-done.8
  43.1 0.0 copy-done.9
  43.2 1.4 shard_map.123
  44.6 0.0 copy-start.7
  44.6 12.7 %all_to_all.90 = bf16[16,8,512]{2,1,0:T(8,128)(2,1)S(1)} all-to-all(bf16[16,8,512]{2,1,0:T(8,128)(2,1)S(1)} %bitcast.49), channel_id=1, replica_groups={{480,448,416,384,352,320,288,256,224,192,160,128,96,64,32,0},{481,449,4..., dimensions={0} | all-to-all | bytes 262144 | tf_op jit(solution)/shard_map/all_to_all | solution.py:446
  57.2 0.0 copy-start.3
  57.3 0.0 copy-done.7
  57.3 0.9 shard_map.124
  58.2 5.7 %all-to-all-start.3 = ((bf16[32,8,512]{2,1,0:T(8,128)(2,1)}), bf16[32,8,512]{2,1,0:T(8,128)(2,1)S(1)}, u32[]{:S(2)}, u32[]{:S(2)}) async-start(bf16[32,8,512]{2,1,0:T(8,128)(2,1)} %bitcast.11), calls=%async_computation.3 | async-start | bytes 524288 | tf_op jit(solution)/shard_map/all_to_all | solution.py:446
  63.8 0.0 copy-done.3
  63.8 0.0 copy-start.4
  63.9 1.0 copy-done.4
  64.9 0.0 copy-start.1
  64.9 0.3 shard_map.125
  65.2 0.0 copy-start.11
  65.2 11.5 %all-to-all-done.3 = bf16[32,8,512]{2,1,0:T(8,128)(2,1)S(1)} async-done(((bf16[32,8,512]{2,1,0:T(8,128)(2,1)}), bf16[32,8,512]{2,1,0:T(8,128)(2,1)S(1)}, u32[]{:S(2)}, u32[]{:S(2)}) %all-to-all-start.3) | async-done | bytes 262176 | tf_op jit(solution)/shard_map/all_to_all | solution.py:446
  76.8 0.0 copy-done.1
  76.8 0.0 copy-done.11
  76.8 1.4 shard_map.126
  78.2 0.0 copy-start.5
  78.2 0.8 copy-done.5
  79.0 16.3 %all_to_all.91 = bf16[32,8,512]{2,1,0:T(8,128)(2,1)S(1)} all-to-all(bf16[32,8,512]{2,1,0:T(8,128)(2,1)S(1)} %bitcast.47), channel_id=1, replica_groups=mesh['gx'=16,'gy'=32] {'gy'}, dimensions={0} | all-to-all | bytes 524288 | tf_op jit(solution)/shard_map/all_to_all | solution.py:446
  95.3 0.5 shard_map.128
  95.8 12.5 %all_to_all.92 = bf16[16,16,256]{2,1,0:T(8,128)(2,1)S(1)} all-to-all(bf16[16,16,256]{2,1,0:T(8,128)(2,1)S(1)} %bitcast.42), channel_id=1, replica_groups={{480,448,416,384,352,320,288,256,224,192,160,128,96,64,32,0},{481,449,4..., dimensions={0} | all-to-all | bytes 262144 | tf_op jit(solution)/shard_map/all_to_all | solution.py:446
  108.3 1.3 shard_map.129
  109.6 12.5 %all_to_all.93 = bf16[16,8,512]{2,1,0:T(8,128)(2,1)S(1)} all-to-all(bf16[16,8,512]{2,1,0:T(8,128)(2,1)S(1)} %bitcast.48), channel_id=1, replica_groups={{480,448,416,384,352,320,288,256,224,192,160,128,96,64,32,0},{481,449,4..., dimensions={0} | all-to-all | bytes 262144 | tf_op jit(solution)/shard_map/all_to_all | solution.py:446
  122.2 0.0 copy-start.6
  122.2 0.9 shard_map.130
  123.1 5.7 %all-to-all-start.7 = ((bf16[32,8,512]{2,1,0:T(8,128)(2,1)}), bf16[32,8,512]{2,1,0:T(8,128)(2,1)S(1)}, u32[]{:S(2)}, u32[]{:S(2)}) async-start(bf16[32,8,512]{2,1,0:T(8,128)(2,1)} %bitcast.23), calls=%async_computation.7 | async-start | bytes 524288 | tf_op jit(solution)/shard_map/all_to_all | solution.py:446
  128.8 0.0 copy-done.6
  128.8 1.0 shard_map.127
  129.7 1.3 shard_map.132
  131.1 10.7 %all-to-all-done.7 = bf16[32,8,512]{2,1,0:T(8,128)(2,1)S(1)} async-done(((bf16[32,8,512]{2,1,0:T(8,128)(2,1)}), bf16[32,8,512]{2,1,0:T(8,128)(2,1)S(1)}, u32[]{:S(2)}, u32[]{:S(2)}) %all-to-all-start.7) | async-done | bytes 262176 | tf_op jit(solution)/shard_map/all_to_all | solution.py:446
  141.7 1.5 %shard_map.131 = bf16[2048,128]{1,0:T(8,128)(2,1)} custom-call(bf16[256,512]{1,0:T(8,128)(2,1)S(1)} %bitcast.39, bf16[4,128,512]{2,1,0:T(8,128)(2,1)S(1)} %get-tuple-element.24.slope_ref, bf16[16,16]{1,0:T(8,128)(2,1)S(1)} %copy-done.11, bf16[256,512]{1,0:T(8,128)(2,1)S(1)} %copy-done.1), custom_call_target="tpu_custom_call" | custom-call | flops 100000000 | bytes 1573376 | tf_op jit(solution)/shard_map/pallas_call | solution.py:429
Async XLA Ops:
  0.6 42.5 %copy-start = (bf16[16,16,4,1,512]{4,2,3,1,0:T(4,128)(2,1)S(1)}, bf16[16,16,4,1,512]{4,2,3,1,0:T(4,128)(2,1)}, u32[]{:S(2)}) copy-start(bf16[16,16,4,1,512]{4,2,3,1,0:T(4,128)(2,1)} %param.11) | copy-start | bytes 3145732
  0.6 1.1 copy-start.2
  2.4 25.8 %copy-start.10 = (bf16[128,256]{1,0:T(8,128)(2,1)S(1)}, bf16[128,256]{1,0:T(8,128)(2,1)}, u32[]{:S(2)}) copy-start(bf16[128,256]{1,0:T(8,128)(2,1)} %constant.24.clone.table_ref) | copy-start | bytes 196612
  28.6 14.6 %copy-start.8 = (bf16[256,128]{1,0:T(8,128)(2,1)S(1)}, bf16[256,128]{1,0:T(8,128)(2,1)}, u32[]{:S(2)}) copy-start(bf16[256,128]{1,0:T(8,128)(2,1)} %constant.27.clone.x_bwd_ref) | copy-start | bytes 196612
  28.6 14.6 %copy-start.9 = (bf16[256,128]{1,0:T(8,128)(2,1)S(1)}, bf16[256,128]{1,0:T(8,128)(2,1)}, u32[]{:S(2)}) copy-start(bf16[256,128]{1,0:T(8,128)(2,1)} %constant.26.clone.x_fwd_ref) | copy-start | bytes 196612
  44.6 12.7 %copy-start.7 = (bf16[256,128]{1,0:T(8,128)(2,1)S(1)}, bf16[256,128]{1,0:T(8,128)(2,1)}, u32[]{:S(2)}) copy-start(bf16[256,128]{1,0:T(8,128)(2,1)} %constant.25.clone.table_ref) | copy-start | bytes 196612
  57.2 6.6 %copy-start.3 = (bf16[1,4,16,8,4,128]{5,4,3,2,1,0:T(4,128)(2,1)S(1)}, bf16[1,4,16,8,4,128]{5,4,3,2,1,0:T(4,128)(2,1)}, u32[]{:S(2)}) copy-start(bf16[1,4,16,8,4,128]{5,4,3,2,1,0:T(4,128)(2,1)} %param.10) | copy-start | bytes 1572868
  58.2 18.6 %all-to-all-start.3 = ((bf16[32,8,512]{2,1,0:T(8,128)(2,1)}), bf16[32,8,512]{2,1,0:T(8,128)(2,1)S(1)}, u32[]{:S(2)}, u32[]{:S(2)}) async-start(bf16[32,8,512]{2,1,0:T(8,128)(2,1)} %bitcast.11), calls=%async_computation.3 | async-start | bytes 524288 | tf_op jit(solution)/shard_map/all_to_all | solution.py:446
  63.8 1.0 copy-start.4
  64.9 11.9 %copy-start.1 = (bf16[256,512]{1,0:T(8,128)(2,1)S(1)}, bf16[256,512]{1,0:T(8,128)(2,1)}, u32[]{:S(2)}) copy-start(bf16[256,512]{1,0:T(8,128)(2,1)} %constant.23.clone.zt_bwd_ref.zt_fwd_ref) | copy-start | bytes 786436
  65.2 11.5 %copy-start.11 = (bf16[16,16]{1,0:T(8,128)(2,1)S(1)}, bf16[16,16]{1,0:T(8,128)(2,1)}, u32[]{:S(2)}) copy-start(bf16[16,16]{1,0:T(8,128)(2,1)} %point_ref.3) | copy-start | bytes 1540
  78.2 0.8 copy-start.5
  122.2 6.6 %copy-start.6 = (bf16[4,128,512]{2,1,0:T(8,128)(2,1)S(1)}, bf16[4,128,512]{2,1,0:T(8,128)(2,1)}, u32[]{:S(2)}) copy-start(bf16[4,128,512]{2,1,0:T(8,128)(2,1)} %copy-done.5) | copy-start | bytes 1572868
  123.1 18.6 %all-to-all-start.7 = ((bf16[32,8,512]{2,1,0:T(8,128)(2,1)}), bf16[32,8,512]{2,1,0:T(8,128)(2,1)S(1)}, u32[]{:S(2)}, u32[]{:S(2)}) async-start(bf16[32,8,512]{2,1,0:T(8,128)(2,1)} %bitcast.23), calls=%async_computation.7 | async-start | bytes 524288 | tf_op jit(solution)/shard_map/all_to_all | solution.py:446

commit v4 on v2

--- a/solution.py
+++ b/solution.py
@@ -159,10 +159,26 @@
     )
 
 
-def open_kernel(field_ref, zt_fwd_ref, out_ref, wide, spread):
+def build_zt(table):
+    shape = (MZ, Z)
+    turns = lax.broadcasted_iota(jnp.int32, shape, 0) * lax.broadcasted_iota(jnp.int32, shape, 1)
+    angle = (turns & (Z - 1)).astype(F32) * (2.0 * math.pi / Z)
+    cosine = jnp.cos(angle)
+    sine = jnp.sin(angle)
+    real = (cosine, -sine, -cosine, sine)
+    imag = (-sine, -cosine, sine, cosine)
+    for kt in range(T):
+        for p, part in enumerate((real, imag)):
+            row = (kt * 2 + p) * MZ
+            for t in range(T):
+                table[row : row + MZ, t * Z : (t + 1) * Z] = part[kt * t % T].astype(BF16)
+
+
+def open_kernel(field_ref, out_ref, wide, spread, table):
+    build_zt(table)
     wide[...] = field_ref[...].astype(F32)
     for y in range(YL):
-        put_modes(spread, y, cells_of(wide, y).astype(BF16), zt_fwd_ref[...])
+        put_modes(spread, y, cells_of(wide, y).astype(BF16), table[...])
     pack(spread, out_ref)
 
 
@@ -232,7 +248,7 @@
         )
 
     zero = jnp.zeros((C, 8, LANES), F32)
-    mix_real, mix_imag = lax.fori_loop(0, C, add, (zero, zero))
+    mix_real, mix_imag = lax.fori_loop(0, C, add, (zero, zero), unroll=4)
     scale = scale_ref[0]
     from_spectrum(
         (mix_real * scale).reshape(C * 8, LANES),
@@ -251,16 +267,20 @@
     x_bwd_ref,
     s_real_ref,
     s_imag_ref,
+    layer_ref,
     out_ref,
     grad_hbm,
+    layer_hbm,
     real_ref,
     imag_ref,
     back_real,
     back_imag,
     spread,
     grad,
-    sem,
+    sems,
 ):
+    send_layer = pltpu.make_async_copy(layer_ref, layer_hbm, sems.at[0])
+    send_layer.start()
     real, imag = to_spectrum(in_ref, x_fwd_ref)
     real_ref[...] = real
     imag_ref[...] = imag
@@ -276,9 +296,9 @@
         grad[c] = both.reshape(C * 2 * 8, LANES).astype(BF16)
         return carry
 
-    lax.fori_loop(0, C, outer, 0)
-    send = pltpu.make_async_copy(grad, grad_hbm, sem)
-    send.start()
+    lax.fori_loop(0, C, outer, 0, unroll=4)
+    send_grad = pltpu.make_async_copy(grad, grad_hbm, sems.at[1])
+    send_grad.start()
 
     def one(c, carry):
         a_real = real_ref[...].reshape(C, 8, LANES)
@@ -289,10 +309,11 @@
         back_imag[row, :] = jnp.sum(a_imag * w_real - a_real * w_imag, 0)
         return carry
 
-    lax.fori_loop(0, C, one, 0)
+    lax.fori_loop(0, C, one, 0, unroll=4)
     scale = scale_ref[0]
     from_spectrum(back_real[...] * scale, back_imag[...] * scale, x_bwd_ref, out_ref, spread)
-    send.wait()
+    send_layer.wait()
+    send_grad.wait()
 
 
 def y_backward_kernel(in_ref, table_ref, out_ref):
@@ -319,12 +340,10 @@
     zt_fwd_ref,
     out_ref,
     slope_ref,
-    layer_hbm,
+    layer_ref,
     wide,
     other,
     spread,
-    layer,
-    sem,
 ):
     point = point_table(point_ref, False)
     unpack(in_ref, spread)
@@ -336,13 +355,10 @@
         value, slope = gelu_parts(pre)
         put_cells(wide, y, value)
         slope_ref[y] = (cells_of(other, y) * slope).astype(BF16)
-    layer[...] = wide[...].astype(BF16)
-    send = pltpu.make_async_copy(layer, layer_hbm, sem)
-    send.start()
+    layer_ref[...] = wide[...].astype(BF16)
     for y in range(YL):
         put_modes(spread, y, slope_ref[y], zt_fwd_ref[...])
     pack(spread, out_ref)
-    send.wait()
 
 
 def close_kernel(in_ref, slope_ref, point_ref, zt_bwd_ref, out_hbm, spread, wide, out, sems):
@@ -410,9 +426,9 @@
     )
 
 
-def open_stage(field, zt_fwd):
-    scratch = [vmem(WIDE), vmem(ZT_SPREAD)]
-    return call(open_kernel, [shaped(ZT)], [field, zt_fwd], scratch)
+def open_stage(field):
+    scratch = [vmem(WIDE), vmem(ZT_SPREAD), vmem((T * 2 * MZ, T * Z), BF16)]
+    return call(open_kernel, [shaped(ZT)], [field], scratch)
 
 
 def y_forward_stage(block, y_fwd):
@@ -434,26 +450,24 @@
 
 
 def cell_stage(block, field, cotangent, point_weight, zt_bwd, zt_fwd):
-    scratch = [vmem(WIDE), vmem(WIDE), vmem(ZT_SPREAD), vmem(WIDE, BF16)]
-    scratch.append(pltpu.SemaphoreType.DMA)
     return call(
         cell_kernel,
         [shaped(ZT), shaped(CELLS), shaped(WIDE)],
         [block, field, cotangent, point_weight, zt_bwd, zt_fwd],
-        scratch,
-        far_outs=(2,),
-    )
-
-
-def back_stage(block, weight, scale, x_fwd, x_bwd, spec_real, spec_imag):
-    scratch = [vmem(PARTS)] * 4 + [vmem(X_SPREAD), vmem(GRAD, BF16), pltpu.SemaphoreType.DMA]
+        [vmem(WIDE), vmem(WIDE), vmem(ZT_SPREAD)],
+    )
+
+
+def back_stage(block, weight, scale, x_fwd, x_bwd, spec_real, spec_imag, layer):
+    scratch = [vmem(PARTS)] * 4 + [vmem(X_SPREAD), vmem(GRAD, BF16)]
+    scratch.append(pltpu.SemaphoreType.DMA((2,)))
     return call(
         back_kernel,
-        [shaped(AFTER_X), shaped(GRAD)],
-        [block, weight, scale, x_fwd, x_bwd, spec_real, spec_imag],
+        [shaped(AFTER_X), shaped(GRAD), shaped(WIDE)],
+        [block, weight, scale, x_fwd, x_bwd, spec_real, spec_imag, layer],
         scratch,
         scalars=(2,),
-        far_outs=(1,),
+        far_outs=(1, 2),
     )
 
 
@@ -475,17 +489,17 @@
     kz = lax.axis_index("gy")
     scale = (jnp.where(kz == 0, 1.0, 2.0).astype(F32) / float(X * Y * Z * T)).reshape(1)
 
-    opened = open_stage(field, zt_fwd)
+    opened = open_stage(field)
     opened, scale = lax.optimization_barrier((opened, scale))
     halved = y_forward_stage(exchange(opened, "gy"), y_fwd)
     mixed, spec_real, spec_imag = mix_stage(exchange(halved, "gx"), weight, scale, x_fwd, x_bwd)
     along_y = y_backward_stage(exchange(mixed, "gx"), y_bwd)
-    turned, slope, layer_out = cell_stage(
+    turned, slope, layer = cell_stage(
         exchange(along_y, "gy"), field, cotan, point_weight, zt_bwd, zt_fwd
     )
     halved = y_forward_stage(exchange(turned, "gy"), y_fwd)
-    back, grad_spectral = back_stage(
-        exchange(halved, "gx"), weight, scale, x_fwd, x_bwd, spec_real, spec_imag
+    back, grad_spectral, layer_out = back_stage(
+        exchange(halved, "gx"), weight, scale, x_fwd, x_bwd, spec_real, spec_imag, layer
     )
     along_y = y_backward_stage(exchange(back, "gx"), y_bwd)
     grad_field = close_stage(exchange(along_y, "gy"), slope, point_weight, zt_bwd)

time: 143 us -> 142 us (level)
  no operation moved by 1% of the time
where the time goes in v4:
time: 142 us; the launch traced here: 141 us
  blocking collectives  131 us (92%)
  Pallas kernels  7.78 us (5%)
    all_to_all x8, blocking collectives, exchange(): lax.all_to_all(block, axis, split_axis=0, concat_axis=0, axis_index_group...  131 us
    pallas_call x9, Pallas kernels, call(): pl.pallas_call(kernel, out_shape=outs[0] if single else tuple(outs), in_s...  7.78 us

profile of v4, /device:TPU:8, one launch (start us, length us, event | category | flops | bytes accessed | tf_op | source)
XLA Modules:
  0.0 141.1 jit_solution(8184569371506647184)
XLA Ops:
  0.6 0.0 copy-start
  0.6 0.0 copy-start.2
  0.7 1.1 copy-done.2
  1.8 0.6 shard_map.121
  2.4 0.0 copy-start.8
  2.4 25.8 %all_to_all.88 = bf16[32,8,512]{2,1,0:T(8,128)(2,1)S(1)} all-to-all(bf16[32,8,512]{2,1,0:T(8,128)(2,1)S(1)} %bitcast.35), channel_id=1, replica_groups=mesh['gx'=16,'gy'=32] {'gy'}, dimensions={0} | all-to-all | bytes 524288 | tf_op jit(solution)/shard_map/all_to_all | solution.py:424
  28.1 0.0 copy-done.8
  28.1 0.5 shard_map.122
  28.6 0.0 copy-start.6
  28.6 0.0 copy-start.7
  28.6 14.5 %all_to_all.89 = bf16[16,16,256]{2,1,0:T(8,128)(2,1)S(1)} all-to-all(bf16[16,16,256]{2,1,0:T(8,128)(2,1)S(1)} %bitcast.47), channel_id=1, replica_groups={{480,448,416,384,352,320,288,256,224,192,160,128,96,64,32,0},{481,449,4..., dimensions={0} | all-to-all | bytes 262144 | tf_op jit(solution)/shard_map/all_to_all | solution.py:424
  43.1 0.0 copy-done
  43.1 0.0 copy-done.6
  43.1 0.0 copy-done.7
  43.2 0.0 copy-start.4
  43.2 1.3 shard_map.123
  44.5 0.0 copy-start.5
  44.5 12.7 %all_to_all.90 = bf16[16,8,512]{2,1,0:T(8,128)(2,1)S(1)} all-to-all(bf16[16,8,512]{2,1,0:T(8,128)(2,1)S(1)} %bitcast.51), channel_id=1, replica_groups={{480,448,416,384,352,320,288,256,224,192,160,128,96,64,32,0},{481,449,4..., dimensions={0} | all-to-all | bytes 262144 | tf_op jit(solution)/shard_map/all_to_all | solution.py:424
  57.2 0.0 copy-start.3
  57.2 0.0 copy-done.5
  57.2 0.2 shard_map.124
  57.4 0.0 copy-start.1
  57.4 0.0 copy-start.9
  57.4 18.5 %all_to_all.91 = bf16[32,8,512]{2,1,0:T(8,128)(2,1)S(1)} all-to-all(bf16[32,8,512]{2,1,0:T(8,128)(2,1)S(1)} %bitcast.40), channel_id=1, replica_groups=mesh['gx'=16,'gy'=32] {'gy'}, dimensions={0} | all-to-all | bytes 524288 | tf_op jit(solution)/shard_map/all_to_all | solution.py:424
  75.9 0.0 copy-done.4
  75.9 0.0 copy-done.3
  75.9 0.0 copy-done.1
  75.9 0.0 copy-done.9
  75.9 1.5 %shard_map.125 = (bf16[256,512]{1,0:T(8,128)(2,1)S(1)}, bf16[4,128,512]{2,1,0:T(8,128)(2,1)S(1)}, bf16[2048,128]{1,0:T(8,128)(2,1)S(1)}) custom-call(bf16[256,512]{1,0:T(8,128)(2,1)S(1)} %bitcast.36, bf16[2048,128]{1,0:T(8,128)(2,1)S(1)} %bitcast.34, bf16[2048,128]{1,0:T(8,128)(2,1)S(1)} %bitcast.42, bf16[16,16]{1,0:T(8,128)(2,1)S(1)} %copy-done.9, ...), custom_call_target="tpu_custom_call" | custom-call | flops 100000000 | bytes 3146240 | tf_op jit(solution)/shard_map/pallas_call | solution.py:407
  77.4 16.4 %all_to_all.92 = bf16[32,8,512]{2,1,0:T(8,128)(2,1)S(1)} all-to-all(bf16[32,8,512]{2,1,0:T(8,128)(2,1)S(1)} %bitcast.49), channel_id=1, replica_groups=mesh['gx'=16,'gy'=32] {'gy'}, dimensions={0} | all-to-all | bytes 524288 | tf_op jit(solution)/shard_map/all_to_all | solution.py:424
  93.8 0.5 shard_map.126
  94.3 12.5 %all_to_all.93 = bf16[16,16,256]{2,1,0:T(8,128)(2,1)S(1)} all-to-all(bf16[16,16,256]{2,1,0:T(8,128)(2,1)S(1)} %bitcast.45), channel_id=1, replica_groups={{480,448,416,384,352,320,288,256,224,192,160,128,96,64,32,0},{481,449,4..., dimensions={0} | all-to-all | bytes 262144 | tf_op jit(solution)/shard_map/all_to_all | solution.py:424
  106.8 1.6 %shard_map.127 = (bf16[128,512]{1,0:T(8,128)(2,1)S(1)}, bf16[16,256,128]{2,1,0:T(8,128)(2,1)}, bf16[2048,128]{1,0:T(8,128)(2,1)}) custom-call(bf16[256,256]{1,0:T(8,128)(2,1)S(1)} %bitcast.43, bf16[16,256,128]{2,1,0:T(8,128)(2,1)S(1)} %bitcast.32, f32[1]{0:T(128)} %bitcast.1.scale_ref, bf16[256,128]{1,0:T(8,128)(2,1)S(1)} %copy-done.7, ...), custom_call_target="tpu_custom_call" | custom-call | flops 100000000 | bytes 3670020 | tf_op jit(solution)/shard_map/pallas_call | solution.py:407
  108.4 12.5 %all_to_all.94 = bf16[16,8,512]{2,1,0:T(8,128)(2,1)S(1)} all-to-all(bf16[16,8,512]{2,1,0:T(8,128)(2,1)S(1)} %bitcast.50), channel_id=1, replica_groups={{480,448,416,384,352,320,288,256,224,192,160,128,96,64,32,0},{481,449,4..., dimensions={0} | all-to-all | bytes 262144 | tf_op jit(solution)/shard_map/all_to_all | solution.py:424
  120.9 0.2 shard_map.128
  121.1 18.4 %all_to_all.95 = bf16[32,8,512]{2,1,0:T(8,128)(2,1)S(1)} all-to-all(bf16[32,8,512]{2,1,0:T(8,128)(2,1)S(1)} %bitcast.38), channel_id=1, replica_groups=mesh['gx'=16,'gy'=32] {'gy'}, dimensions={0} | all-to-all | bytes 524288 | tf_op jit(solution)/shard_map/all_to_all | solution.py:424
  139.6 1.5 %shard_map.129 = bf16[2048,128]{1,0:T(8,128)(2,1)} custom-call(bf16[256,512]{1,0:T(8,128)(2,1)S(1)} %bitcast.41, bf16[4,128,512]{2,1,0:T(8,128)(2,1)S(1)} %get-tuple-element.23.slope_ref, bf16[16,16]{1,0:T(8,128)(2,1)S(1)} %copy-done.9, bf16[256,512]{1,0:T(8,128)(2,1)S(1)} %copy-done.1), custom_call_target="tpu_custom_call" | custom-call | flops 100000000 | bytes 1573376 | tf_op jit(solution)/shard_map/pallas_call | solution.py:407
Async XLA Ops:
  0.6 42.5 %copy-start = (bf16[16,16,4,1,512]{4,2,3,1,0:T(4,128)(2,1)S(1)}, bf16[16,16,4,1,512]{4,2,3,1,0:T(4,128)(2,1)}, u32[]{:S(2)}) copy-start(bf16[16,16,4,1,512]{4,2,3,1,0:T(4,128)(2,1)} %param.11) | copy-start | bytes 3145732
  0.6 1.1 copy-start.2
  2.4 25.8 %copy-start.8 = (bf16[128,256]{1,0:T(8,128)(2,1)S(1)}, bf16[128,256]{1,0:T(8,128)(2,1)}, u32[]{:S(2)}) copy-start(bf16[128,256]{1,0:T(8,128)(2,1)} %constant.24.clone.table_ref) | copy-start | bytes 196612
  28.6 14.6 %copy-start.6 = (bf16[256,128]{1,0:T(8,128)(2,1)S(1)}, bf16[256,128]{1,0:T(8,128)(2,1)}, u32[]{:S(2)}) copy-start(bf16[256,128]{1,0:T(8,128)(2,1)} %constant.27.clone.x_bwd_ref) | copy-start | bytes 196612
  28.6 14.6 %copy-start.7 = (bf16[256,128]{1,0:T(8,128)(2,1)S(1)}, bf16[256,128]{1,0:T(8,128)(2,1)}, u32[]{:S(2)}) copy-start(bf16[256,128]{1,0:T(8,128)(2,1)} %constant.26.clone.x_fwd_ref) | copy-start | bytes 196612
  43.2 32.8 %copy-start.4 = (bf16[1,4,16,8,4,128]{5,4,3,2,1,0:T(4,128)(2,1)S(1)}, bf16[1,4,16,8,4,128]{5,4,3,2,1,0:T(4,128)(2,1)}, u32[]{:S(2)}) copy-start(bf16[1,4,16,8,4,128]{5,4,3,2,1,0:T(4,128)(2,1)} %param.13) | copy-start | bytes 1572868
  44.5 12.7 %copy-start.5 = (bf16[256,128]{1,0:T(8,128)(2,1)S(1)}, bf16[256,128]{1,0:T(8,128)(2,1)}, u32[]{:S(2)}) copy-start(bf16[256,128]{1,0:T(8,128)(2,1)} %constant.25.clone.table_ref) | copy-start | bytes 196612
  57.2 18.8 %copy-start.3 = (bf16[1,4,16,8,4,128]{5,4,3,2,1,0:T(4,128)(2,1)S(1)}, bf16[1,4,16,8,4,128]{5,4,3,2,1,0:T(4,128)(2,1)}, u32[]{:S(2)}) copy-start(bf16[1,4,16,8,4,128]{5,4,3,2,1,0:T(4,128)(2,1)} %param.10) | copy-start | bytes 1572868
  57.4 18.5 %copy-start.1 = (bf16[256,512]{1,0:T(8,128)(2,1)S(1)}, bf16[256,512]{1,0:T(8,128)(2,1)}, u32[]{:S(2)}) copy-start(bf16[256,512]{1,0:T(8,128)(2,1)} %constant.23.clone.zt_bwd_ref.zt_fwd_ref) | copy-start | bytes 786436
  57.4 18.5 %copy-start.9 = (bf16[16,16]{1,0:T(8,128)(2,1)S(1)}, bf16[16,16]{1,0:T(8,128)(2,1)}, u32[]{:S(2)}) copy-start(bf16[16,16]{1,0:T(8,128)(2,1)} %point_ref.3) | copy-start | bytes 1540

commit v5 on v4

--- a/solution.py
+++ b/solution.py
@@ -22,7 +22,7 @@
 YL = Y // GY
 JL = MY // GX
 LANES = 128
-GX_ORDER = list(range(GX))[::-1]
+GX_ORDER = [z * 8 + x * 2 + core for z in (1, 0) for x in (2, 0, 3, 1) for core in (1, 0)]
 
 F32 = jnp.float32
 BF16 = jnp.bfloat16
@@ -341,11 +341,13 @@
     out_ref,
     slope_ref,
     layer_ref,
+    back_ref,
     wide,
     other,
     spread,
 ):
     point = point_table(point_ref, False)
+    back_ref[...] = point_table(point_ref, True)
     unpack(in_ref, spread)
     modes = [modes_of(spread, y).astype(BF16) for y in range(YL)]
     wide[...] = field_ref[...].astype(F32)
@@ -362,7 +364,7 @@
 
 
 def close_kernel(in_ref, slope_ref, point_ref, zt_bwd_ref, out_hbm, spread, wide, out, sems):
-    point = point_table(point_ref, True)
+    point = point_ref[...]
     unpack(in_ref, spread)
     for y in range(YL):
         modes = modes_of(spread, y).astype(BF16)
@@ -452,7 +454,7 @@
 def cell_stage(block, field, cotangent, point_weight, zt_bwd, zt_fwd):
     return call(
         cell_kernel,
-        [shaped(ZT), shaped(CELLS), shaped(WIDE)],
+        [shaped(ZT), shaped(CELLS), shaped(WIDE), shaped((C * XL, C * XL))],
         [block, field, cotangent, point_weight, zt_bwd, zt_fwd],
         [vmem(WIDE), vmem(WIDE), vmem(ZT_SPREAD)],
     )
@@ -471,11 +473,11 @@
     )
 
 
-def close_stage(block, slope, point_weight, zt_bwd):
+def close_stage(block, slope, point_back, zt_bwd):
     return call(
         close_kernel,
         [shaped(WIDE)],
-        [block, slope, point_weight, zt_bwd],
+        [block, slope, point_back, zt_bwd],
         [vmem(ZT_SPREAD), vmem(WIDE), vmem(WIDE, BF16), pltpu.SemaphoreType.DMA((T,))],
         far_outs=(0,),
     )
@@ -494,7 +496,7 @@
     halved = y_forward_stage(exchange(opened, "gy"), y_fwd)
     mixed, spec_real, spec_imag = mix_stage(exchange(halved, "gx"), weight, scale, x_fwd, x_bwd)
     along_y = y_backward_stage(exchange(mixed, "gx"), y_bwd)
-    turned, slope, layer = cell_stage(
+    turned, slope, layer, point_back = cell_stage(
         exchange(along_y, "gy"), field, cotan, point_weight, zt_bwd, zt_fwd
     )
     halved = y_forward_stage(exchange(turned, "gy"), y_fwd)
@@ -502,7 +504,7 @@
         exchange(halved, "gx"), weight, scale, x_fwd, x_bwd, spec_real, spec_imag, layer
     )
     along_y = y_backward_stage(exchange(back, "gx"), y_bwd)
-    grad_field = close_stage(exchange(along_y, "gy"), slope, point_weight, zt_bwd)
+    grad_field = close_stage(exchange(along_y, "gy"), slope, point_back, zt_bwd)
 
     grad_spectral = (
         grad_spectral.reshape(C, C, 4, JL, LANES)

time: 142 us -> 141 us (level)
  the two profiles are of different devices: /device:TPU:8 before, /device:TPU:2 now
where the time goes in v5:
time: 141 us; the launch traced here: 140 us
  blocking collectives  131 us (93%)
  Pallas kernels  7.72 us (5%)
    all_to_all x8, blocking collectives, exchange(): lax.all_to_all(block, axis, split_axis=0, concat_axis=0, axis_index_group...  131 us
    pallas_call x9, Pallas kernels, call(): pl.pallas_call(kernel, out_shape=outs[0] if single else tuple(outs), in_s...  7.72 us

profile of v5, /device:TPU:2, one launch (start us, length us, event | category | flops | bytes accessed | tf_op | source)
XLA Modules:
  0.0 140.4 jit_solution(2413525167351428826)
XLA Ops:
  0.6 0.0 copy-start
  0.6 0.0 copy-start.2
  0.7 1.1 copy-done.2
  1.8 0.6 shard_map.121
  2.4 0.0 copy-start.8
  2.4 26.1 %all_to_all.88 = bf16[32,8,512]{2,1,0:T(8,128)(2,1)S(1)} all-to-all(bf16[32,8,512]{2,1,0:T(8,128)(2,1)S(1)} %bitcast.35), channel_id=1, replica_groups=mesh['gx'=16,'gy'=32] {'gy'}, dimensions={0} | all-to-all | bytes 524288 | tf_op jit(solution)/shard_map/all_to_all | solution.py:426
  28.5 0.0 copy-done.8
  28.5 0.5 shard_map.122
  29.0 0.0 copy-start.6
  29.0 0.0 copy-start.7
  29.0 13.7 %all_to_all.89 = bf16[16,16,256]{2,1,0:T(8,128)(2,1)S(1)} all-to-all(bf16[16,16,256]{2,1,0:T(8,128)(2,1)S(1)} %bitcast.47), channel_id=1, replica_groups={{416,384,288,256,480,448,352,320,160,128,32,0,224,192,96,64},{417,385,2..., dimensions={0} | all-to-all | bytes 262144 | tf_op jit(solution)/shard_map/all_to_all | solution.py:426
  42.6 0.0 copy-done
  42.6 0.0 copy-done.6
  42.6 0.0 copy-done.7
  42.7 0.0 copy-start.4
  42.7 1.3 shard_map.123
  44.0 0.0 copy-start.5
  44.0 12.7 %all_to_all.90 = bf16[16,8,512]{2,1,0:T(8,128)(2,1)S(1)} all-to-all(bf16[16,8,512]{2,1,0:T(8,128)(2,1)S(1)} %bitcast.51), channel_id=1, replica_groups={{416,384,288,256,480,448,352,320,160,128,32,0,224,192,96,64},{417,385,2..., dimensions={0} | all-to-all | bytes 262144 | tf_op jit(solution)/shard_map/all_to_all | solution.py:426
  56.7 0.0 copy-start.3
  56.7 0.0 copy-done.5
  56.7 0.2 shard_map.124
  56.9 0.0 copy-start.1
  56.9 0.0 copy-start.9
  56.9 18.7 %all_to_all.91 = bf16[32,8,512]{2,1,0:T(8,128)(2,1)S(1)} all-to-all(bf16[32,8,512]{2,1,0:T(8,128)(2,1)S(1)} %bitcast.41), channel_id=1, replica_groups=mesh['gx'=16,'gy'=32] {'gy'}, dimensions={0} | all-to-all | bytes 524288 | tf_op jit(solution)/shard_map/all_to_all | solution.py:426
  75.6 0.0 copy-done.4
  75.6 0.0 copy-done.3
  75.6 0.0 copy-done.1
  75.6 0.0 copy-done.9
  75.6 1.6 %shard_map.125 = (bf16[256,512]{1,0:T(8,128)(2,1)S(1)}, bf16[4,128,512]{2,1,0:T(8,128)(2,1)S(1)}, bf16[2048,128]{1,0:T(8,128)(2,1)S(1)}, bf16[128,128]{1,0:T(8,128)(2,1)S(1)}) custom-call(bf16[256,512]{1,0:T(8,128)(2,1)S(1)} %bitcast.36, bf16[2048,128]{1,0:T(8,128)(2,1)S(1)} %bitcast.34, bf16[2048,128]{1,0:T(8,128)(2,1)S(1)} %bitcast.42, ...), custom_call_target="tpu_custom_call" | custom-call | flops 100000000 | bytes 3179008 | tf_op jit(solution)/shard_map/pallas_call | solution.py:409
  77.2 16.2 %all_to_all.92 = bf16[32,8,512]{2,1,0:T(8,128)(2,1)S(1)} all-to-all(bf16[32,8,512]{2,1,0:T(8,128)(2,1)S(1)} %bitcast.49), channel_id=1, replica_groups=mesh['gx'=16,'gy'=32] {'gy'}, dimensions={0} | all-to-all | bytes 524288 | tf_op jit(solution)/shard_map/all_to_all | solution.py:426
  93.3 0.5 shard_map.126
  93.8 12.4 %all_to_all.93 = bf16[16,16,256]{2,1,0:T(8,128)(2,1)S(1)} all-to-all(bf16[16,16,256]{2,1,0:T(8,128)(2,1)S(1)} %bitcast.45), channel_id=1, replica_groups={{416,384,288,256,480,448,352,320,160,128,32,0,224,192,96,64},{417,385,2..., dimensions={0} | all-to-all | bytes 262144 | tf_op jit(solution)/shard_map/all_to_all | solution.py:426
  106.2 1.6 %shard_map.127 = (bf16[128,512]{1,0:T(8,128)(2,1)S(1)}, bf16[16,256,128]{2,1,0:T(8,128)(2,1)}, bf16[2048,128]{1,0:T(8,128)(2,1)}) custom-call(bf16[256,256]{1,0:T(8,128)(2,1)S(1)} %bitcast.43, bf16[16,256,128]{2,1,0:T(8,128)(2,1)S(1)} %bitcast.32, f32[1]{0:T(128)} %bitcast.1.scale_ref, bf16[256,128]{1,0:T(8,128)(2,1)S(1)} %copy-done.7, ...), custom_call_target="tpu_custom_call" | custom-call | flops 100000000 | bytes 3670020 | tf_op jit(solution)/shard_map/pallas_call | solution.py:409
  107.7 12.5 %all_to_all.94 = bf16[16,8,512]{2,1,0:T(8,128)(2,1)S(1)} all-to-all(bf16[16,8,512]{2,1,0:T(8,128)(2,1)S(1)} %bitcast.50), channel_id=1, replica_groups={{416,384,288,256,480,448,352,320,160,128,32,0,224,192,96,64},{417,385,2..., dimensions={0} | all-to-all | bytes 262144 | tf_op jit(solution)/shard_map/all_to_all | solution.py:426
  120.3 0.2 shard_map.128
  120.5 18.5 %all_to_all.95 = bf16[32,8,512]{2,1,0:T(8,128)(2,1)S(1)} all-to-all(bf16[32,8,512]{2,1,0:T(8,128)(2,1)S(1)} %bitcast.39), channel_id=1, replica_groups=mesh['gx'=16,'gy'=32] {'gy'}, dimensions={0} | all-to-all | bytes 524288 | tf_op jit(solution)/shard_map/all_to_all | solution.py:426
  139.0 1.4 shard_map.129
Async XLA Ops:
  0.6 42.0 %copy-start = (bf16[16,16,4,1,512]{4,2,3,1,0:T(4,128)(2,1)S(1)}, bf16[16,16,4,1,512]{4,2,3,1,0:T(4,128)(2,1)}, u32[]{:S(2)}) copy-start(bf16[16,16,4,1,512]{4,2,3,1,0:T(4,128)(2,1)} %param.11) | copy-start | bytes 3145732
  0.6 1.1 copy-start.2
  2.4 26.1 %copy-start.8 = (bf16[128,256]{1,0:T(8,128)(2,1)S(1)}, bf16[128,256]{1,0:T(8,128)(2,1)}, u32[]{:S(2)}) copy-start(bf16[128,256]{1,0:T(8,128)(2,1)} %constant.24.clone.table_ref) | copy-start | bytes 196612
  29.0 13.7 %copy-start.6 = (bf16[256,128]{1,0:T(8,128)(2,1)S(1)}, bf16[256,128]{1,0:T(8,128)(2,1)}, u32[]{:S(2)}) copy-start(bf16[256,128]{1,0:T(8,128)(2,1)} %constant.27.clone.x_bwd_ref) | copy-start | bytes 196612
  29.0 13.7 %copy-start.7 = (bf16[256,128]{1,0:T(8,128)(2,1)S(1)}, bf16[256,128]{1,0:T(8,128)(2,1)}, u32[]{:S(2)}) copy-start(bf16[256,128]{1,0:T(8,128)(2,1)} %constant.26.clone.x_fwd_ref) | copy-start | bytes 196612
  42.7 32.9 %copy-start.4 = (bf16[1,4,16,8,4,128]{5,4,3,2,1,0:T(4,128)(2,1)S(1)}, bf16[1,4,16,8,4,128]{5,4,3,2,1,0:T(4,128)(2,1)}, u32[]{:S(2)}) copy-start(bf16[1,4,16,8,4,128]{5,4,3,2,1,0:T(4,128)(2,1)} %param.13) | copy-start | bytes 1572868
  44.0 12.7 %copy-start.5 = (bf16[256,128]{1,0:T(8,128)(2,1)S(1)}, bf16[256,128]{1,0:T(8,128)(2,1)}, u32[]{:S(2)}) copy-start(bf16[256,128]{1,0:T(8,128)(2,1)} %constant.25.clone.table_ref) | copy-start | bytes 196612
  56.7 18.9 %copy-start.3 = (bf16[1,4,16,8,4,128]{5,4,3,2,1,0:T(4,128)(2,1)S(1)}, bf16[1,4,16,8,4,128]{5,4,3,2,1,0:T(4,128)(2,1)}, u32[]{:S(2)}) copy-start(bf16[1,4,16,8,4,128]{5,4,3,2,1,0:T(4,128)(2,1)} %param.10) | copy-start | bytes 1572868
  56.9 18.7 %copy-start.1 = (bf16[256,512]{1,0:T(8,128)(2,1)S(1)}, bf16[256,512]{1,0:T(8,128)(2,1)}, u32[]{:S(2)}) copy-start(bf16[256,512]{1,0:T(8,128)(2,1)} %constant.23.clone.zt_bwd_ref.zt_fwd_ref) | copy-start | bytes 786436
  56.9 18.7 %copy-start.9 = (bf16[16,16]{1,0:T(8,128)(2,1)S(1)}, bf16[16,16]{1,0:T(8,128)(2,1)}, u32[]{:S(2)}) copy-start(bf16[16,16]{1,0:T(8,128)(2,1)} %point_ref.1) | copy-start | bytes 1540

commit v6 on v5

--- a/solution.py
+++ b/solution.py
@@ -174,9 +174,17 @@
                 table[row : row + MZ, t * Z : (t + 1) * Z] = part[kt * t % T].astype(BF16)
 
 
-def open_kernel(field_ref, out_ref, wide, spread, table):
+def open_kernel(field_hbm, out_ref, field, wide, spread, table, sems):
+    copies = []
+    for t in range(T):
+        rows = pl.ds(t * C * XL * YL, C * XL * YL)
+        copies.append(pltpu.make_async_copy(field_hbm.at[rows], field.at[rows], sems.at[t]))
+        copies[t].start()
     build_zt(table)
-    wide[...] = field_ref[...].astype(F32)
+    for t in range(T):
+        rows = pl.ds(t * C * XL * YL, C * XL * YL)
+        copies[t].wait()
+        wide[rows, :] = field[rows, :].astype(F32)
     for y in range(YL):
         put_modes(spread, y, cells_of(wide, y).astype(BF16), table[...])
     pack(spread, out_ref)
@@ -392,17 +400,21 @@
 
 WIDE = (ROWS, Z)
 GRAD = (C, C * 2 * 8, LANES)
+GRANT = 16 * 1024 * 1024
+OPEN_GRANT = 64 * 1024 * 1024 - 448 * 1024
 
 
 def vmem(shape, dtype=F32):
     return pltpu.VMEM(shape, dtype)
 
 
-def call(kernel, outs, operands, scratch=(), scalars=(), far_outs=(), flops=10**8):
+def call(kernel, outs, operands, scratch=(), scalars=(), far=(), far_outs=(), grant=GRANT):
     near = pl.BlockSpec(memory_space=pltpu.VMEM)
     smem = pl.BlockSpec(memory_space=pltpu.SMEM)
     anywhere = pl.BlockSpec(memory_space=pltpu.HBM)
-    specs = [smem if i in scalars else near for i in range(len(operands))]
+    specs = [
+        smem if i in scalars else anywhere if i in far else near for i in range(len(operands))
+    ]
     out_specs = tuple(anywhere if i in far_outs else near for i in range(len(outs)))
     single = len(outs) == 1
     moved = sum(math.prod(o.shape) * o.dtype.itemsize for o in list(outs) + list(operands))
@@ -412,8 +424,8 @@
         in_specs=specs,
         out_specs=out_specs[0] if single else out_specs,
         scratch_shapes=list(scratch),
-        cost_estimate=pl.CostEstimate(flops=flops, bytes_accessed=moved, transcendentals=0),
-        compiler_params=pltpu.CompilerParams(vmem_limit_bytes=16 * 1024 * 1024),
+        cost_estimate=pl.CostEstimate(flops=10**8, bytes_accessed=moved, transcendentals=0),
+        compiler_params=pltpu.CompilerParams(vmem_limit_bytes=grant),
     )(*operands)
 
 
@@ -429,8 +441,9 @@
 
 
 def open_stage(field):
-    scratch = [vmem(WIDE), vmem(ZT_SPREAD), vmem((T * 2 * MZ, T * Z), BF16)]
-    return call(open_kernel, [shaped(ZT)], [field], scratch)
+    scratch = [vmem(WIDE, BF16), vmem(WIDE), vmem(ZT_SPREAD), vmem((T * 2 * MZ, T * Z), BF16)]
+    scratch.append(pltpu.SemaphoreType.DMA((T,)))
+    return call(open_kernel, [shaped(ZT)], [field], scratch, far=(0,), grant=OPEN_GRANT)
 
 
 def y_forward_stage(block, y_fwd):

time: 141 us -> 142 us (level)
  Pallas kernels: 7.72 us -> 9.48 us
    pallas_call x9, Pallas kernels: 7.72 us -> 9.48 us  [call(): pl.pallas_call(kernel, out_shape=outs[0] if single else tuple(outs), in_s...]
where the time goes in v6:
time: 142 us; the launch traced here: 141 us
  blocking collectives  131 us (92%)
  Pallas kernels  9.48 us (7%)
    all_to_all x8, blocking collectives, exchange(): lax.all_to_all(block, axis, split_axis=0, concat_axis=0, axis_index_group...  131 us
    pallas_call x9, Pallas kernels, call(): pl.pallas_call(kernel, out_shape=outs[0] if single else tuple(outs), in_s...  9.48 us

profile of v6, /device:TPU:2, one launch (start us, length us, event | category | flops | bytes accessed | tf_op | source)
XLA Modules:
  0.0 141.2 jit_solution(4615181379841820424)
XLA Ops:
  0.6 0.0 copy-start.7
  0.6 2.3 %shard_map.121 = bf16[256,512]{1,0:T(8,128)(2,1)} custom-call(bf16[2048,128]{1,0:T(8,128)(2,1)} %bitcast.33), custom_call_target="tpu_custom_call" | custom-call | flops 100000000 | bytes 786432 | tf_op jit(solution)/shard_map/pallas_call | solution.py:421
  3.0 0.0 copy-start
  3.0 26.3 %all_to_all.88 = bf16[32,8,512]{2,1,0:T(8,128)(2,1)S(1)} all-to-all(bf16[32,8,512]{2,1,0:T(8,128)(2,1)} %bitcast.51), channel_id=1, replica_groups=mesh['gx'=16,'gy'=32] {'gy'}, dimensions={0} | all-to-all | bytes 524288 | tf_op jit(solution)/shard_map/all_to_all | solution.py:438
  29.3 0.0 copy-done.7
  29.3 0.5 shard_map.122
  29.8 0.0 copy-start.5
  29.8 0.0 copy-start.6
  29.8 13.7 %all_to_all.89 = bf16[16,16,256]{2,1,0:T(8,128)(2,1)S(1)} all-to-all(bf16[16,16,256]{2,1,0:T(8,128)(2,1)S(1)} %bitcast.46), channel_id=1, replica_groups={{416,384,288,256,480,448,352,320,160,128,32,0,224,192,96,64},{417,385,2..., dimensions={0} | all-to-all | bytes 262144 | tf_op jit(solution)/shard_map/all_to_all | solution.py:438
  43.5 0.0 copy-done
  43.5 0.0 copy-done.5
  43.5 0.0 copy-done.6
  43.5 0.0 copy-start.3
  43.5 1.3 shard_map.123
  44.8 0.0 copy-start.4
  44.8 12.7 %all_to_all.90 = bf16[16,8,512]{2,1,0:T(8,128)(2,1)S(1)} all-to-all(bf16[16,8,512]{2,1,0:T(8,128)(2,1)S(1)} %bitcast.50), channel_id=1, replica_groups={{416,384,288,256,480,448,352,320,160,128,32,0,224,192,96,64},{417,385,2..., dimensions={0} | all-to-all | bytes 262144 | tf_op jit(solution)/shard_map/all_to_all | solution.py:438
  57.5 0.0 copy-start.2
  57.5 0.0 copy-done.4
  57.5 0.2 shard_map.124
  57.7 0.0 copy-start.1
  57.7 0.0 copy-start.8
  57.7 18.7 %all_to_all.91 = bf16[32,8,512]{2,1,0:T(8,128)(2,1)S(1)} all-to-all(bf16[32,8,512]{2,1,0:T(8,128)(2,1)S(1)} %bitcast.40), channel_id=1, replica_groups=mesh['gx'=16,'gy'=32] {'gy'}, dimensions={0} | all-to-all | bytes 524288 | tf_op jit(solution)/shard_map/all_to_all | solution.py:438
  76.4 0.0 copy-done.3
  76.4 0.0 copy-done.2
  76.4 0.0 copy-done.1
  76.4 0.0 copy-done.8
  76.4 1.6 %shard_map.125 = (bf16[256,512]{1,0:T(8,128)(2,1)S(1)}, bf16[4,128,512]{2,1,0:T(8,128)(2,1)S(1)}, bf16[2048,128]{1,0:T(8,128)(2,1)S(1)}, bf16[128,128]{1,0:T(8,128)(2,1)S(1)}) custom-call(bf16[256,512]{1,0:T(8,128)(2,1)S(1)} %bitcast.35, bf16[2048,128]{1,0:T(8,128)(2,1)S(1)} %bitcast.34, bf16[2048,128]{1,0:T(8,128)(2,1)S(1)} %bitcast.41, ...), custom_call_target="tpu_custom_call" | custom-call | flops 100000000 | bytes 3179008 | tf_op jit(solution)/shard_map/pallas_call | solution.py:421
  78.0 16.2 %all_to_all.92 = bf16[32,8,512]{2,1,0:T(8,128)(2,1)S(1)} all-to-all(bf16[32,8,512]{2,1,0:T(8,128)(2,1)S(1)} %bitcast.48), channel_id=1, replica_groups=mesh['gx'=16,'gy'=32] {'gy'}, dimensions={0} | all-to-all | bytes 524288 | tf_op jit(solution)/shard_map/all_to_all | solution.py:438
  94.2 0.5 shard_map.126
  94.6 12.4 %all_to_all.93 = bf16[16,16,256]{2,1,0:T(8,128)(2,1)S(1)} all-to-all(bf16[16,16,256]{2,1,0:T(8,128)(2,1)S(1)} %bitcast.44), channel_id=1, replica_groups={{416,384,288,256,480,448,352,320,160,128,32,0,224,192,96,64},{417,385,2..., dimensions={0} | all-to-all | bytes 262144 | tf_op jit(solution)/shard_map/all_to_all | solution.py:438
  107.0 1.6 %shard_map.127 = (bf16[128,512]{1,0:T(8,128)(2,1)S(1)}, bf16[16,256,128]{2,1,0:T(8,128)(2,1)}, bf16[2048,128]{1,0:T(8,128)(2,1)}) custom-call(bf16[256,256]{1,0:T(8,128)(2,1)S(1)} %bitcast.42, bf16[16,256,128]{2,1,0:T(8,128)(2,1)S(1)} %bitcast.32, f32[1]{0:T(128)} %bitcast.1.scale_ref, bf16[256,128]{1,0:T(8,128)(2,1)S(1)} %copy-done.6, ...), custom_call_target="tpu_custom_call" | custom-call | flops 100000000 | bytes 3670020 | tf_op jit(solution)/shard_map/pallas_call | solution.py:421
  108.6 12.5 %all_to_all.94 = bf16[16,8,512]{2,1,0:T(8,128)(2,1)S(1)} all-to-all(bf16[16,8,512]{2,1,0:T(8,128)(2,1)S(1)} %bitcast.49), channel_id=1, replica_groups={{416,384,288,256,480,448,352,320,160,128,32,0,224,192,96,64},{417,385,2..., dimensions={0} | all-to-all | bytes 262144 | tf_op jit(solution)/shard_map/all_to_all | solution.py:438
  121.1 0.2 shard_map.128
  121.3 18.5 %all_to_all.95 = bf16[32,8,512]{2,1,0:T(8,128)(2,1)S(1)} all-to-all(bf16[32,8,512]{2,1,0:T(8,128)(2,1)S(1)} %bitcast.38), channel_id=1, replica_groups=mesh['gx'=16,'gy'=32] {'gy'}, dimensions={0} | all-to-all | bytes 524288 | tf_op jit(solution)/shard_map/all_to_all | solution.py:438
  139.9 1.4 shard_map.129
Async XLA Ops:
  0.6 28.7 %copy-start.7 = (bf16[128,256]{1,0:T(8,128)(2,1)S(1)}, bf16[128,256]{1,0:T(8,128)(2,1)}, u32[]{:S(2)}) copy-start(bf16[128,256]{1,0:T(8,128)(2,1)} %constant.24.clone.table_ref) | copy-start | bytes 196612
  3.0 40.5 %copy-start = (bf16[16,16,4,1,512]{4,2,3,1,0:T(4,128)(2,1)S(1)}, bf16[16,16,4,1,512]{4,2,3,1,0:T(4,128)(2,1)}, u32[]{:S(2)}) copy-start(bf16[16,16,4,1,512]{4,2,3,1,0:T(4,128)(2,1)} %param.11) | copy-start | bytes 3145732
  29.8 13.7 %copy-start.5 = (bf16[256,128]{1,0:T(8,128)(2,1)S(1)}, bf16[256,128]{1,0:T(8,128)(2,1)}, u32[]{:S(2)}) copy-start(bf16[256,128]{1,0:T(8,128)(2,1)} %constant.27.clone.x_bwd_ref) | copy-start | bytes 196612
  29.8 13.7 %copy-start.6 = (bf16[256,128]{1,0:T(8,128)(2,1)S(1)}, bf16[256,128]{1,0:T(8,128)(2,1)}, u32[]{:S(2)}) copy-start(bf16[256,128]{1,0:T(8,128)(2,1)} %constant.26.clone.x_fwd_ref) | copy-start | bytes 196612
  43.5 32.9 %copy-start.3 = (bf16[1,4,16,8,4,128]{5,4,3,2,1,0:T(4,128)(2,1)S(1)}, bf16[1,4,16,8,4,128]{5,4,3,2,1,0:T(4,128)(2,1)}, u32[]{:S(2)}) copy-start(bf16[1,4,16,8,4,128]{5,4,3,2,1,0:T(4,128)(2,1)} %param.13) | copy-start | bytes 1572868
  44.8 12.7 %copy-start.4 = (bf16[256,128]{1,0:T(8,128)(2,1)S(1)}, bf16[256,128]{1,0:T(8,128)(2,1)}, u32[]{:S(2)}) copy-start(bf16[256,128]{1,0:T(8,128)(2,1)} %constant.25.clone.table_ref) | copy-start | bytes 196612
  57.5 18.9 %copy-start.2 = (bf16[1,4,16,8,4,128]{5,4,3,2,1,0:T(4,128)(2,1)S(1)}, bf16[1,4,16,8,4,128]{5,4,3,2,1,0:T(4,128)(2,1)}, u32[]{:S(2)}) copy-start(bf16[1,4,16,8,4,128]{5,4,3,2,1,0:T(4,128)(2,1)} %param.10) | copy-start | bytes 1572868
  57.7 18.7 %copy-start.1 = (bf16[256,512]{1,0:T(8,128)(2,1)S(1)}, bf16[256,512]{1,0:T(8,128)(2,1)}, u32[]{:S(2)}) copy-start(bf16[256,512]{1,0:T(8,128)(2,1)} %constant.23.clone.zt_bwd_ref.zt_fwd_ref) | copy-start | bytes 786436
  57.7 18.7 %copy-start.8 = (bf16[16,16]{1,0:T(8,128)(2,1)S(1)}, bf16[16,16]{1,0:T(8,128)(2,1)}, u32[]{:S(2)}) copy-start(bf16[16,16]{1,0:T(8,128)(2,1)} %point_ref.1) | copy-start | bytes 1540

commit v7 on v5

--- a/solution.py
+++ b/solution.py
@@ -132,12 +132,14 @@
 
 def pack(spread_ref, out_ref):
     for k in range(spread_ref.shape[0]):
-        out_ref[:, k * LANES : (k + 1) * LANES] = spread_ref[k].astype(BF16)
+        block = spread_ref[k, 0 : out_ref.shape[0], :]
+        out_ref[:, k * LANES : (k + 1) * LANES] = block.astype(BF16)
 
 
 def unpack(in_ref, spread_ref):
     for k in range(spread_ref.shape[0]):
-        spread_ref[k] = in_ref[:, k * LANES : (k + 1) * LANES].astype(F32)
+        block = in_ref[:, k * LANES : (k + 1) * LANES].astype(F32)
+        spread_ref[k, 0 : in_ref.shape[0], :] = block
 
 
 def put_modes(spread_ref, y, cells, zt_fwd):
@@ -176,7 +178,7 @@
 
 def open_kernel(field_ref, out_ref, wide, spread, table):
     build_zt(table)
-    wide[...] = field_ref[...].astype(F32)
+    wide[0:ROWS, :] = field_ref[...].astype(F32)
     for y in range(YL):
         put_modes(spread, y, cells_of(wide, y).astype(BF16), table[...])
     pack(spread, out_ref)
@@ -350,14 +352,14 @@
     back_ref[...] = point_table(point_ref, True)
     unpack(in_ref, spread)
     modes = [modes_of(spread, y).astype(BF16) for y in range(YL)]
-    wide[...] = field_ref[...].astype(F32)
-    other[...] = cotangent_ref[...].astype(F32)
+    wide[0:ROWS, :] = field_ref[...].astype(F32)
+    other[0:ROWS, :] = cotangent_ref[...].astype(F32)
     for y in range(YL):
         pre = dot(modes[y], zt_bwd_ref[...], 0, 0) + dot(point, cells_of(wide, y).astype(BF16))
         value, slope = gelu_parts(pre)
         put_cells(wide, y, value)
         slope_ref[y] = (cells_of(other, y) * slope).astype(BF16)
-    layer_ref[...] = wide[...].astype(BF16)
+    layer_ref[...] = wide[0:ROWS, :].astype(BF16)
     for y in range(YL):
         put_modes(spread, y, slope_ref[y], zt_fwd_ref[...])
     pack(spread, out_ref)
@@ -383,14 +385,15 @@
 ZT = (MZ * YL * 2, T * LANES)
 AFTER_Y = (GX * XL * 2, 2 * LANES)
 AFTER_X = (GX * JL * 2, T * LANES)
-ZT_SPREAD = (T, MZ * YL * 2, LANES)
-Y_SPREAD = (2, GX * XL * 2, LANES)
-X_SPREAD = (T, GX * JL * 2, LANES)
+ZT_SPREAD = (T, MZ * YL * 2 + 16, LANES)
+Y_SPREAD = (2, GX * XL * 2 + 16, LANES)
+X_SPREAD = (T, GX * JL * 2 + 16, LANES)
 CELLS = (YL, C * XL, T * Z)
 PARTS = (C * 8, LANES)
 
 
 WIDE = (ROWS, Z)
+WIDE_SPREAD = (ROWS + 16, Z)
 GRAD = (C, C * 2 * 8, LANES)
 
 
@@ -429,7 +432,7 @@
 
 
 def open_stage(field):
-    scratch = [vmem(WIDE), vmem(ZT_SPREAD), vmem((T * 2 * MZ, T * Z), BF16)]
+    scratch = [vmem(WIDE_SPREAD), vmem(ZT_SPREAD), vmem((T * 2 * MZ, T * Z), BF16)]
     return call(open_kernel, [shaped(ZT)], [field], scratch)
 
 
@@ -456,7 +459,7 @@
         cell_kernel,
         [shaped(ZT), shaped(CELLS), shaped(WIDE), shaped((C * XL, C * XL))],
         [block, field, cotangent, point_weight, zt_bwd, zt_fwd],
-        [vmem(WIDE), vmem(WIDE), vmem(ZT_SPREAD)],
+        [vmem(WIDE_SPREAD), vmem(WIDE_SPREAD), vmem(ZT_SPREAD)],
     )
 
 
@@ -478,7 +481,7 @@
         close_kernel,
         [shaped(WIDE)],
         [block, slope, point_back, zt_bwd],
-        [vmem(ZT_SPREAD), vmem(WIDE), vmem(WIDE, BF16), pltpu.SemaphoreType.DMA((T,))],
+        [vmem(ZT_SPREAD), vmem(WIDE_SPREAD), vmem(WIDE, BF16), pltpu.SemaphoreType.DMA((T,))],
         far_outs=(0,),
     )
 

time: 141 us -> 141 us (level)
  no operation moved by 1% of the time
where the time goes in v7:
time: 141 us; the launch traced here: 140 us
  blocking collectives  131 us (93%)
  Pallas kernels  7.71 us (5%)
    all_to_all x8, blocking collectives, exchange(): lax.all_to_all(block, axis, split_axis=0, concat_axis=0, axis_index_group...  131 us
    pallas_call x9, Pallas kernels, call(): pl.pallas_call(kernel, out_shape=outs[0] if single else tuple(outs), in_s...  7.71 us

profile of v7, /device:TPU:2, one launch (start us, length us, event | category | flops | bytes accessed | tf_op | source)
XLA Modules:
  0.0 140.4 jit_solution(18325908321542932856)
XLA Ops:
  0.6 0.0 copy-start
  0.6 0.0 copy-start.2
  0.7 1.1 copy-done.2
  1.8 0.6 shard_map.121
  2.4 0.0 copy-start.8
  2.4 26.1 %all_to_all.88 = bf16[32,8,512]{2,1,0:T(8,128)(2,1)S(1)} all-to-all(bf16[32,8,512]{2,1,0:T(8,128)(2,1)S(1)} %bitcast.35), channel_id=1, replica_groups=mesh['gx'=16,'gy'=32] {'gy'}, dimensions={0} | all-to-all | bytes 524288 | tf_op jit(solution)/shard_map/all_to_all | solution.py:429
  28.5 0.0 copy-done.8
  28.5 0.5 shard_map.122
  29.0 0.0 copy-start.6
  29.0 0.0 copy-start.7
  29.0 13.7 %all_to_all.89 = bf16[16,16,256]{2,1,0:T(8,128)(2,1)S(1)} all-to-all(bf16[16,16,256]{2,1,0:T(8,128)(2,1)S(1)} %bitcast.47), channel_id=1, replica_groups={{416,384,288,256,480,448,352,320,160,128,32,0,224,192,96,64},{417,385,2..., dimensions={0} | all-to-all | bytes 262144 | tf_op jit(solution)/shard_map/all_to_all | solution.py:429
  42.6 0.0 copy-done
  42.6 0.0 copy-done.6
  42.6 0.0 copy-done.7
  42.7 0.0 copy-start.4
  42.7 1.3 shard_map.123
  44.0 0.0 copy-start.5
  44.0 12.7 %all_to_all.90 = bf16[16,8,512]{2,1,0:T(8,128)(2,1)S(1)} all-to-all(bf16[16,8,512]{2,1,0:T(8,128)(2,1)S(1)} %bitcast.51), channel_id=1, replica_groups={{416,384,288,256,480,448,352,320,160,128,32,0,224,192,96,64},{417,385,2..., dimensions={0} | all-to-all | bytes 262144 | tf_op jit(solution)/shard_map/all_to_all | solution.py:429
  56.7 0.0 copy-start.3
  56.7 0.0 copy-done.5
  56.7 0.2 shard_map.124
  56.9 0.0 copy-start.1
  56.9 0.0 copy-start.9
  56.9 18.7 %all_to_all.91 = bf16[32,8,512]{2,1,0:T(8,128)(2,1)S(1)} all-to-all(bf16[32,8,512]{2,1,0:T(8,128)(2,1)S(1)} %bitcast.41), channel_id=1, replica_groups=mesh['gx'=16,'gy'=32] {'gy'}, dimensions={0} | all-to-all | bytes 524288 | tf_op jit(solution)/shard_map/all_to_all | solution.py:429
  75.6 0.0 copy-done.4
  75.6 0.0 copy-done.3
  75.6 0.0 copy-done.1
  75.6 0.0 copy-done.9
  75.6 1.6 %shard_map.125 = (bf16[256,512]{1,0:T(8,128)(2,1)S(1)}, bf16[4,128,512]{2,1,0:T(8,128)(2,1)S(1)}, bf16[2048,128]{1,0:T(8,128)(2,1)S(1)}, bf16[128,128]{1,0:T(8,128)(2,1)S(1)}) custom-call(bf16[256,512]{1,0:T(8,128)(2,1)S(1)} %bitcast.36, bf16[2048,128]{1,0:T(8,128)(2,1)S(1)} %bitcast.34, bf16[2048,128]{1,0:T(8,128)(2,1)S(1)} %bitcast.42, ...), custom_call_target="tpu_custom_call" | custom-call | flops 100000000 | bytes 3179008 | tf_op jit(solution)/shard_map/pallas_call | solution.py:412
  77.2 16.2 %all_to_all.92 = bf16[32,8,512]{2,1,0:T(8,128)(2,1)S(1)} all-to-all(bf16[32,8,512]{2,1,0:T(8,128)(2,1)S(1)} %bitcast.49), channel_id=1, replica_groups=mesh['gx'=16,'gy'=32] {'gy'}, dimensions={0} | all-to-all | bytes 524288 | tf_op jit(solution)/shard_map/all_to_all | solution.py:429
  93.3 0.5 shard_map.126
  93.8 12.4 %all_to_all.93 = bf16[16,16,256]{2,1,0:T(8,128)(2,1)S(1)} all-to-all(bf16[16,16,256]{2,1,0:T(8,128)(2,1)S(1)} %bitcast.45), channel_id=1, replica_groups={{416,384,288,256,480,448,352,320,160,128,32,0,224,192,96,64},{417,385,2..., dimensions={0} | all-to-all | bytes 262144 | tf_op jit(solution)/shard_map/all_to_all | solution.py:429
  106.2 1.6 %shard_map.127 = (bf16[128,512]{1,0:T(8,128)(2,1)S(1)}, bf16[16,256,128]{2,1,0:T(8,128)(2,1)}, bf16[2048,128]{1,0:T(8,128)(2,1)}) custom-call(bf16[256,256]{1,0:T(8,128)(2,1)S(1)} %bitcast.43, bf16[16,256,128]{2,1,0:T(8,128)(2,1)S(1)} %bitcast.32, f32[1]{0:T(128)} %bitcast.1.scale_ref, bf16[256,128]{1,0:T(8,128)(2,1)S(1)} %copy-done.7, ...), custom_call_target="tpu_custom_call" | custom-call | flops 100000000 | bytes 3670020 | tf_op jit(solution)/shard_map/pallas_call | solution.py:412
  107.7 12.5 %all_to_all.94 = bf16[16,8,512]{2,1,0:T(8,128)(2,1)S(1)} all-to-all(bf16[16,8,512]{2,1,0:T(8,128)(2,1)S(1)} %bitcast.50), channel_id=1, replica_groups={{416,384,288,256,480,448,352,320,160,128,32,0,224,192,96,64},{417,385,2..., dimensions={0} | all-to-all | bytes 262144 | tf_op jit(solution)/shard_map/all_to_all | solution.py:429
  120.3 0.2 shard_map.128
  120.5 18.6 %all_to_all.95 = bf16[32,8,512]{2,1,0:T(8,128)(2,1)S(1)} all-to-all(bf16[32,8,512]{2,1,0:T(8,128)(2,1)S(1)} %bitcast.39), channel_id=1, replica_groups=mesh['gx'=16,'gy'=32] {'gy'}, dimensions={0} | all-to-all | bytes 524288 | tf_op jit(solution)/shard_map/all_to_all | solution.py:429
  139.0 1.4 shard_map.129
Async XLA Ops:
  0.6 42.0 %copy-start = (bf16[16,16,4,1,512]{4,2,3,1,0:T(4,128)(2,1)S(1)}, bf16[16,16,4,1,512]{4,2,3,1,0:T(4,128)(2,1)}, u32[]{:S(2)}) copy-start(bf16[16,16,4,1,512]{4,2,3,1,0:T(4,128)(2,1)} %param.11) | copy-start | bytes 3145732
  0.6 1.1 copy-start.2
  2.4 26.1 %copy-start.8 = (bf16[128,256]{1,0:T(8,128)(2,1)S(1)}, bf16[128,256]{1,0:T(8,128)(2,1)}, u32[]{:S(2)}) copy-start(bf16[128,256]{1,0:T(8,128)(2,1)} %constant.24.clone.table_ref) | copy-start | bytes 196612
  29.0 13.7 %copy-start.6 = (bf16[256,128]{1,0:T(8,128)(2,1)S(1)}, bf16[256,128]{1,0:T(8,128)(2,1)}, u32[]{:S(2)}) copy-start(bf16[256,128]{1,0:T(8,128)(2,1)} %constant.27.clone.x_bwd_ref) | copy-start | bytes 196612
  29.0 13.7 %copy-start.7 = (bf16[256,128]{1,0:T(8,128)(2,1)S(1)}, bf16[256,128]{1,0:T(8,128)(2,1)}, u32[]{:S(2)}) copy-start(bf16[256,128]{1,0:T(8,128)(2,1)} %constant.26.clone.x_fwd_ref) | copy-start | bytes 196612
  42.7 32.9 %copy-start.4 = (bf16[1,4,16,8,4,128]{5,4,3,2,1,0:T(4,128)(2,1)S(1)}, bf16[1,4,16,8,4,128]{5,4,3,2,1,0:T(4,128)(2,1)}, u32[]{:S(2)}) copy-start(bf16[1,4,16,8,4,128]{5,4,3,2,1,0:T(4,128)(2,1)} %param.13) | copy-start | bytes 1572868
  44.0 12.7 %copy-start.5 = (bf16[256,128]{1,0:T(8,128)(2,1)S(1)}, bf16[256,128]{1,0:T(8,128)(2,1)}, u32[]{:S(2)}) copy-start(bf16[256,128]{1,0:T(8,128)(2,1)} %constant.25.clone.table_ref) | copy-start | bytes 196612
  56.7 18.9 %copy-start.3 = (bf16[1,4,16,8,4,128]{5,4,3,2,1,0:T(4,128)(2,1)S(1)}, bf16[1,4,16,8,4,128]{5,4,3,2,1,0:T(4,128)(2,1)}, u32[]{:S(2)}) copy-start(bf16[1,4,16,8,4,128]{5,4,3,2,1,0:T(4,128)(2,1)} %param.10) | copy-start | bytes 1572868
  56.9 18.7 %copy-start.1 = (bf16[256,512]{1,0:T(8,128)(2,1)S(1)}, bf16[256,512]{1,0:T(8,128)(2,1)}, u32[]{:S(2)}) copy-start(bf16[256,512]{1,0:T(8,128)(2,1)} %constant.23.clone.zt_bwd_ref.zt_fwd_ref) | copy-start | bytes 786436
  56.9 18.7 %copy-start.9 = (bf16[16,16]{1,0:T(8,128)(2,1)S(1)}, bf16[16,16]{1,0:T(8,128)(2,1)}, u32[]{:S(2)}) copy-start(bf16[16,16]{1,0:T(8,128)(2,1)} %point_ref.1) | copy-start | bytes 1540

commit v8 on v7

--- a/solution.py
+++ b/solution.py
@@ -250,7 +250,7 @@
         )
 
     zero = jnp.zeros((C, 8, LANES), F32)
-    mix_real, mix_imag = lax.fori_loop(0, C, add, (zero, zero), unroll=4)
+    mix_real, mix_imag = lax.fori_loop(0, C, add, (zero, zero), unroll=C)
     scale = scale_ref[0]
     from_spectrum(
         (mix_real * scale).reshape(C * 8, LANES),

time: 141 us -> 141 us (level)
  no operation moved by 1% of the time
where the time goes in v8:
time: 141 us; the launch traced here: 140 us
  blocking collectives  131 us (93%)
  Pallas kernels  7.58 us (5%)
    all_to_all x8, blocking collectives, exchange(): lax.all_to_all(block, axis, split_axis=0, concat_axis=0, axis_index_group...  131 us
    pallas_call x9, Pallas kernels, call(): pl.pallas_call(kernel, out_shape=outs[0] if single else tuple(outs), in_s...  7.58 us

profile of v8, /device:TPU:2, one launch (start us, length us, event | category | flops | bytes accessed | tf_op | source)
XLA Modules:
  0.0 140.3 jit_solution(11038849355304858797)
XLA Ops:
  0.6 0.0 copy-start
  0.6 0.0 copy-start.2
  0.7 1.1 copy-done.2
  1.8 0.6 shard_map.121
  2.4 0.0 copy-start.8
  2.4 26.1 %all_to_all.88 = bf16[32,8,512]{2,1,0:T(8,128)(2,1)S(1)} all-to-all(bf16[32,8,512]{2,1,0:T(8,128)(2,1)S(1)} %bitcast.35), channel_id=1, replica_groups=mesh['gx'=16,'gy'=32] {'gy'}, dimensions={0} | all-to-all | bytes 524288 | tf_op jit(solution)/shard_map/all_to_all | solution.py:429
  28.5 0.0 copy-done.8
  28.5 0.5 shard_map.122
  29.0 0.0 copy-start.6
  29.0 0.0 copy-start.7
  29.0 13.7 %all_to_all.89 = bf16[16,16,256]{2,1,0:T(8,128)(2,1)S(1)} all-to-all(bf16[16,16,256]{2,1,0:T(8,128)(2,1)S(1)} %bitcast.47), channel_id=1, replica_groups={{416,384,288,256,480,448,352,320,160,128,32,0,224,192,96,64},{417,385,2..., dimensions={0} | all-to-all | bytes 262144 | tf_op jit(solution)/shard_map/all_to_all | solution.py:429
  42.6 0.0 copy-done
  42.6 0.0 copy-done.6
  42.6 0.0 copy-done.7
  42.7 0.0 copy-start.4
  42.7 1.2 shard_map.123
  43.9 0.0 copy-start.5
  43.9 12.7 %all_to_all.90 = bf16[16,8,512]{2,1,0:T(8,128)(2,1)S(1)} all-to-all(bf16[16,8,512]{2,1,0:T(8,128)(2,1)S(1)} %bitcast.51), channel_id=1, replica_groups={{416,384,288,256,480,448,352,320,160,128,32,0,224,192,96,64},{417,385,2..., dimensions={0} | all-to-all | bytes 262144 | tf_op jit(solution)/shard_map/all_to_all | solution.py:429
  56.5 0.0 copy-start.3
  56.5 0.0 copy-done.5
  56.5 0.2 shard_map.124
  56.8 0.0 copy-start.1
  56.8 0.0 copy-start.9
  56.8 18.7 %all_to_all.91 = bf16[32,8,512]{2,1,0:T(8,128)(2,1)S(1)} all-to-all(bf16[32,8,512]{2,1,0:T(8,128)(2,1)S(1)} %bitcast.41), channel_id=1, replica_groups=mesh['gx'=16,'gy'=32] {'gy'}, dimensions={0} | all-to-all | bytes 524288 | tf_op jit(solution)/shard_map/all_to_all | solution.py:429
  75.4 0.0 copy-done.4
  75.4 0.0 copy-done.3
  75.4 0.0 copy-done.1
  75.5 0.0 copy-done.9
  75.5 1.6 %shard_map.125 = (bf16[256,512]{1,0:T(8,128)(2,1)S(1)}, bf16[4,128,512]{2,1,0:T(8,128)(2,1)S(1)}, bf16[2048,128]{1,0:T(8,128)(2,1)S(1)}, bf16[128,128]{1,0:T(8,128)(2,1)S(1)}) custom-call(bf16[256,512]{1,0:T(8,128)(2,1)S(1)} %bitcast.36, bf16[2048,128]{1,0:T(8,128)(2,1)S(1)} %bitcast.34, bf16[2048,128]{1,0:T(8,128)(2,1)S(1)} %bitcast.42, ...), custom_call_target="tpu_custom_call" | custom-call | flops 100000000 | bytes 3179008 | tf_op jit(solution)/shard_map/pallas_call | solution.py:412
  77.0 16.2 %all_to_all.92 = bf16[32,8,512]{2,1,0:T(8,128)(2,1)S(1)} all-to-all(bf16[32,8,512]{2,1,0:T(8,128)(2,1)S(1)} %bitcast.49), channel_id=1, replica_groups=mesh['gx'=16,'gy'=32] {'gy'}, dimensions={0} | all-to-all | bytes 524288 | tf_op jit(solution)/shard_map/all_to_all | solution.py:429
  93.2 0.5 shard_map.126
  93.7 12.4 %all_to_all.93 = bf16[16,16,256]{2,1,0:T(8,128)(2,1)S(1)} all-to-all(bf16[16,16,256]{2,1,0:T(8,128)(2,1)S(1)} %bitcast.45), channel_id=1, replica_groups={{416,384,288,256,480,448,352,320,160,128,32,0,224,192,96,64},{417,385,2..., dimensions={0} | all-to-all | bytes 262144 | tf_op jit(solution)/shard_map/all_to_all | solution.py:429
  106.0 1.6 %shard_map.127 = (bf16[128,512]{1,0:T(8,128)(2,1)S(1)}, bf16[16,256,128]{2,1,0:T(8,128)(2,1)}, bf16[2048,128]{1,0:T(8,128)(2,1)}) custom-call(bf16[256,256]{1,0:T(8,128)(2,1)S(1)} %bitcast.43, bf16[16,256,128]{2,1,0:T(8,128)(2,1)S(1)} %bitcast.32, f32[1]{0:T(128)} %bitcast.1.scale_ref, bf16[256,128]{1,0:T(8,128)(2,1)S(1)} %copy-done.7, ...), custom_call_target="tpu_custom_call" | custom-call | flops 100000000 | bytes 3670020 | tf_op jit(solution)/shard_map/pallas_call | solution.py:412
  107.6 12.5 %all_to_all.94 = bf16[16,8,512]{2,1,0:T(8,128)(2,1)S(1)} all-to-all(bf16[16,8,512]{2,1,0:T(8,128)(2,1)S(1)} %bitcast.50), channel_id=1, replica_groups={{416,384,288,256,480,448,352,320,160,128,32,0,224,192,96,64},{417,385,2..., dimensions={0} | all-to-all | bytes 262144 | tf_op jit(solution)/shard_map/all_to_all | solution.py:429
  120.1 0.2 shard_map.128
  120.4 18.5 %all_to_all.95 = bf16[32,8,512]{2,1,0:T(8,128)(2,1)S(1)} all-to-all(bf16[32,8,512]{2,1,0:T(8,128)(2,1)S(1)} %bitcast.39), channel_id=1, replica_groups=mesh['gx'=16,'gy'=32] {'gy'}, dimensions={0} | all-to-all | bytes 524288 | tf_op jit(solution)/shard_map/all_to_all | solution.py:429
  138.9 1.4 shard_map.129
Async XLA Ops:
  0.6 42.0 %copy-start = (bf16[16,16,4,1,512]{4,2,3,1,0:T(4,128)(2,1)S(1)}, bf16[16,16,4,1,512]{4,2,3,1,0:T(4,128)(2,1)}, u32[]{:S(2)}) copy-start(bf16[16,16,4,1,512]{4,2,3,1,0:T(4,128)(2,1)} %param.11) | copy-start | bytes 3145732
  0.6 1.1 copy-start.2
  2.4 26.1 %copy-start.8 = (bf16[128,256]{1,0:T(8,128)(2,1)S(1)}, bf16[128,256]{1,0:T(8,128)(2,1)}, u32[]{:S(2)}) copy-start(bf16[128,256]{1,0:T(8,128)(2,1)} %constant.24.clone.table_ref) | copy-start | bytes 196612
  29.0 13.7 %copy-start.6 = (bf16[256,128]{1,0:T(8,128)(2,1)S(1)}, bf16[256,128]{1,0:T(8,128)(2,1)}, u32[]{:S(2)}) copy-start(bf16[256,128]{1,0:T(8,128)(2,1)} %constant.27.clone.x_bwd_ref) | copy-start | bytes 196612
  29.0 13.7 %copy-start.7 = (bf16[256,128]{1,0:T(8,128)(2,1)S(1)}, bf16[256,128]{1,0:T(8,128)(2,1)}, u32[]{:S(2)}) copy-start(bf16[256,128]{1,0:T(8,128)(2,1)} %constant.26.clone.x_fwd_ref) | copy-start | bytes 196612
  42.7 32.8 %copy-start.4 = (bf16[1,4,16,8,4,128]{5,4,3,2,1,0:T(4,128)(2,1)S(1)}, bf16[1,4,16,8,4,128]{5,4,3,2,1,0:T(4,128)(2,1)}, u32[]{:S(2)}) copy-start(bf16[1,4,16,8,4,128]{5,4,3,2,1,0:T(4,128)(2,1)} %param.13) | copy-start | bytes 1572868
  43.9 12.7 %copy-start.5 = (bf16[256,128]{1,0:T(8,128)(2,1)S(1)}, bf16[256,128]{1,0:T(8,128)(2,1)}, u32[]{:S(2)}) copy-start(bf16[256,128]{1,0:T(8,128)(2,1)} %constant.25.clone.table_ref) | copy-start | bytes 196612
  56.5 18.9 %copy-start.3 = (bf16[1,4,16,8,4,128]{5,4,3,2,1,0:T(4,128)(2,1)S(1)}, bf16[1,4,16,8,4,128]{5,4,3,2,1,0:T(4,128)(2,1)}, u32[]{:S(2)}) copy-start(bf16[1,4,16,8,4,128]{5,4,3,2,1,0:T(4,128)(2,1)} %param.10) | copy-start | bytes 1572868
  56.8 18.7 %copy-start.1 = (bf16[256,512]{1,0:T(8,128)(2,1)S(1)}, bf16[256,512]{1,0:T(8,128)(2,1)}, u32[]{:S(2)}) copy-start(bf16[256,512]{1,0:T(8,128)(2,1)} %constant.23.clone.zt_bwd_ref.zt_fwd_ref) | copy-start | bytes 786436
  56.8 18.7 %copy-start.9 = (bf16[16,16]{1,0:T(8,128)(2,1)S(1)}, bf16[16,16]{1,0:T(8,128)(2,1)}, u32[]{:S(2)}) copy-start(bf16[16,16]{1,0:T(8,128)(2,1)} %point_ref.1) | copy-start | bytes 1540

commit v9 on v8

--- a/solution.py
+++ b/solution.py
@@ -22,7 +22,7 @@
 YL = Y // GY
 JL = MY // GX
 LANES = 128
-GX_ORDER = [z * 8 + x * 2 + core for z in (1, 0) for x in (2, 0, 3, 1) for core in (1, 0)]
+GX_ORDER = [z * 8 + x * 2 + core for z in (1, 0) for x in (1, 3, 0, 2) for core in (1, 0)]
 
 F32 = jnp.float32
 BF16 = jnp.bfloat16

time: 141 us -> 142 us (level)
  the two profiles are of different devices: /device:TPU:2 before, /device:TPU:8 now
where the time goes in v9:
time: 142 us; the launch traced here: 141 us
  blocking collectives  132 us (93%)
  Pallas kernels  7.57 us (5%)
    all_to_all x8, blocking collectives, exchange(): lax.all_to_all(block, axis, split_axis=0, concat_axis=0, axis_index_group...  132 us
    pallas_call x9, Pallas kernels, call(): pl.pallas_call(kernel, out_shape=outs[0] if single else tuple(outs), in_s...  7.57 us

profile of v9, /device:TPU:8, one launch (start us, length us, event | category | flops | bytes accessed | tf_op | source)
XLA Modules:
  0.0 141.0 jit_solution(12690829185774761781)
XLA Ops:
  0.6 0.0 copy-start
  0.6 0.0 copy-start.2
  0.7 1.1 copy-done.2
  1.8 0.6 shard_map.121
  2.4 0.0 copy-start.8
  2.4 25.8 %all_to_all.88 = bf16[32,8,512]{2,1,0:T(8,128)(2,1)S(1)} all-to-all(bf16[32,8,512]{2,1,0:T(8,128)(2,1)S(1)} %bitcast.35), channel_id=1, replica_groups=mesh['gx'=16,'gy'=32] {'gy'}, dimensions={0} | all-to-all | bytes 524288 | tf_op jit(solution)/shard_map/all_to_all | solution.py:429
  28.1 0.0 copy-done.8
  28.1 0.5 shard_map.122
  28.6 0.0 copy-start.6
  28.6 0.0 copy-start.7
  28.6 15.2 %all_to_all.89 = bf16[16,16,256]{2,1,0:T(8,128)(2,1)S(1)} all-to-all(bf16[16,16,256]{2,1,0:T(8,128)(2,1)S(1)} %bitcast.47), channel_id=1, replica_groups={{352,320,480,448,288,256,416,384,96,64,224,192,32,0,160,128},{353,321,4..., dimensions={0} | all-to-all | bytes 262144 | tf_op jit(solution)/shard_map/all_to_all | solution.py:429
  43.8 0.0 copy-done
  43.8 0.0 copy-done.6
  43.8 0.0 copy-done.7
  43.8 0.0 copy-start.4
  43.8 1.2 shard_map.123
  45.0 0.0 copy-start.5
  45.0 12.7 %all_to_all.90 = bf16[16,8,512]{2,1,0:T(8,128)(2,1)S(1)} all-to-all(bf16[16,8,512]{2,1,0:T(8,128)(2,1)S(1)} %bitcast.51), channel_id=1, replica_groups={{352,320,480,448,288,256,416,384,96,64,224,192,32,0,160,128},{353,321,4..., dimensions={0} | all-to-all | bytes 262144 | tf_op jit(solution)/shard_map/all_to_all | solution.py:429
  57.7 0.0 copy-start.3
  57.7 0.0 copy-done.5
  57.7 0.2 shard_map.124
  57.9 0.0 copy-start.1
  57.9 0.0 copy-start.9
  57.9 18.3 %all_to_all.91 = bf16[32,8,512]{2,1,0:T(8,128)(2,1)S(1)} all-to-all(bf16[32,8,512]{2,1,0:T(8,128)(2,1)S(1)} %bitcast.41), channel_id=1, replica_groups=mesh['gx'=16,'gy'=32] {'gy'}, dimensions={0} | all-to-all | bytes 524288 | tf_op jit(solution)/shard_map/all_to_all | solution.py:429
  76.2 0.0 copy-done.4
  76.2 0.0 copy-done.3
  76.2 0.0 copy-done.1
  76.2 0.0 copy-done.9
  76.3 1.6 %shard_map.125 = (bf16[256,512]{1,0:T(8,128)(2,1)S(1)}, bf16[4,128,512]{2,1,0:T(8,128)(2,1)S(1)}, bf16[2048,128]{1,0:T(8,128)(2,1)S(1)}, bf16[128,128]{1,0:T(8,128)(2,1)S(1)}) custom-call(bf16[256,512]{1,0:T(8,128)(2,1)S(1)} %bitcast.36, bf16[2048,128]{1,0:T(8,128)(2,1)S(1)} %bitcast.34, bf16[2048,128]{1,0:T(8,128)(2,1)S(1)} %bitcast.42, ...), custom_call_target="tpu_custom_call" | custom-call | flops 100000000 | bytes 3179008 | tf_op jit(solution)/shard_map/pallas_call | solution.py:412
  77.8 16.4 %all_to_all.92 = bf16[32,8,512]{2,1,0:T(8,128)(2,1)S(1)} all-to-all(bf16[32,8,512]{2,1,0:T(8,128)(2,1)S(1)} %bitcast.49), channel_id=1, replica_groups=mesh['gx'=16,'gy'=32] {'gy'}, dimensions={0} | all-to-all | bytes 524288 | tf_op jit(solution)/shard_map/all_to_all | solution.py:429
  94.2 0.5 shard_map.126
  94.7 12.5 %all_to_all.93 = bf16[16,16,256]{2,1,0:T(8,128)(2,1)S(1)} all-to-all(bf16[16,16,256]{2,1,0:T(8,128)(2,1)S(1)} %bitcast.45), channel_id=1, replica_groups={{352,320,480,448,288,256,416,384,96,64,224,192,32,0,160,128},{353,321,4..., dimensions={0} | all-to-all | bytes 262144 | tf_op jit(solution)/shard_map/all_to_all | solution.py:429
  107.2 1.6 %shard_map.127 = (bf16[128,512]{1,0:T(8,128)(2,1)S(1)}, bf16[16,256,128]{2,1,0:T(8,128)(2,1)}, bf16[2048,128]{1,0:T(8,128)(2,1)}) custom-call(bf16[256,256]{1,0:T(8,128)(2,1)S(1)} %bitcast.43, bf16[16,256,128]{2,1,0:T(8,128)(2,1)S(1)} %bitcast.32, f32[1]{0:T(128)} %bitcast.1.scale_ref, bf16[256,128]{1,0:T(8,128)(2,1)S(1)} %copy-done.7, ...), custom_call_target="tpu_custom_call" | custom-call | flops 100000000 | bytes 3670020 | tf_op jit(solution)/shard_map/pallas_call | solution.py:412
  108.8 12.5 %all_to_all.94 = bf16[16,8,512]{2,1,0:T(8,128)(2,1)S(1)} all-to-all(bf16[16,8,512]{2,1,0:T(8,128)(2,1)S(1)} %bitcast.50), channel_id=1, replica_groups={{352,320,480,448,288,256,416,384,96,64,224,192,32,0,160,128},{353,321,4..., dimensions={0} | all-to-all | bytes 262144 | tf_op jit(solution)/shard_map/all_to_all | solution.py:429
  121.3 0.2 shard_map.128
  121.5 18.2 %all_to_all.95 = bf16[32,8,512]{2,1,0:T(8,128)(2,1)S(1)} all-to-all(bf16[32,8,512]{2,1,0:T(8,128)(2,1)S(1)} %bitcast.39), channel_id=1, replica_groups=mesh['gx'=16,'gy'=32] {'gy'}, dimensions={0} | all-to-all | bytes 524288 | tf_op jit(solution)/shard_map/all_to_all | solution.py:429
  139.7 1.4 shard_map.129
Async XLA Ops:
  0.6 43.2 %copy-start = (bf16[16,16,4,1,512]{4,2,3,1,0:T(4,128)(2,1)S(1)}, bf16[16,16,4,1,512]{4,2,3,1,0:T(4,128)(2,1)}, u32[]{:S(2)}) copy-start(bf16[16,16,4,1,512]{4,2,3,1,0:T(4,128)(2,1)} %param.11) | copy-start | bytes 3145732
  0.6 1.1 copy-start.2
  2.4 25.8 %copy-start.8 = (bf16[128,256]{1,0:T(8,128)(2,1)S(1)}, bf16[128,256]{1,0:T(8,128)(2,1)}, u32[]{:S(2)}) copy-start(bf16[128,256]{1,0:T(8,128)(2,1)} %constant.24.clone.table_ref) | copy-start | bytes 196612
  28.6 15.2 %copy-start.6 = (bf16[256,128]{1,0:T(8,128)(2,1)S(1)}, bf16[256,128]{1,0:T(8,128)(2,1)}, u32[]{:S(2)}) copy-start(bf16[256,128]{1,0:T(8,128)(2,1)} %constant.27.clone.x_bwd_ref) | copy-start | bytes 196612
  28.6 15.2 %copy-start.7 = (bf16[256,128]{1,0:T(8,128)(2,1)S(1)}, bf16[256,128]{1,0:T(8,128)(2,1)}, u32[]{:S(2)}) copy-start(bf16[256,128]{1,0:T(8,128)(2,1)} %constant.26.clone.x_fwd_ref) | copy-start | bytes 196612
  43.8 32.4 %copy-start.4 = (bf16[1,4,16,8,4,128]{5,4,3,2,1,0:T(4,128)(2,1)S(1)}, bf16[1,4,16,8,4,128]{5,4,3,2,1,0:T(4,128)(2,1)}, u32[]{:S(2)}) copy-start(bf16[1,4,16,8,4,128]{5,4,3,2,1,0:T(4,128)(2,1)} %param.13) | copy-start | bytes 1572868
  45.0 12.7 %copy-start.5 = (bf16[256,128]{1,0:T(8,128)(2,1)S(1)}, bf16[256,128]{1,0:T(8,128)(2,1)}, u32[]{:S(2)}) copy-start(bf16[256,128]{1,0:T(8,128)(2,1)} %constant.25.clone.table_ref) | copy-start | bytes 196612
  57.7 18.5 %copy-start.3 = (bf16[1,4,16,8,4,128]{5,4,3,2,1,0:T(4,128)(2,1)S(1)}, bf16[1,4,16,8,4,128]{5,4,3,2,1,0:T(4,128)(2,1)}, u32[]{:S(2)}) copy-start(bf16[1,4,16,8,4,128]{5,4,3,2,1,0:T(4,128)(2,1)} %param.10) | copy-start | bytes 1572868
  57.9 18.3 %copy-start.1 = (bf16[256,512]{1,0:T(8,128)(2,1)S(1)}, bf16[256,512]{1,0:T(8,128)(2,1)}, u32[]{:S(2)}) copy-start(bf16[256,512]{1,0:T(8,128)(2,1)} %constant.23.clone.zt_bwd_ref.zt_fwd_ref) | copy-start | bytes 786436
  57.9 18.3 %copy-start.9 = (bf16[16,16]{1,0:T(8,128)(2,1)S(1)}, bf16[16,16]{1,0:T(8,128)(2,1)}, u32[]{:S(2)}) copy-start(bf16[16,16]{1,0:T(8,128)(2,1)} %point_ref.1) | copy-start | bytes 1540
